TPU v7x, 256 devices: a whole 4x4x8 slice. The times are simulated.
256 devices in a mesh: tensor: 4 (over z_hi, core), section: 64 (over y, x, z_lo).
Axes of the slice: x: 4, y: 4, z: 8 (z_hi: 2, z_lo: 4; z = z_hi * 4 + z_lo), core: 2. Of those that a mesh axis runs over, the one named last changes fastest.
Arguments:
- prompt_lengths: int32 [2], replicated, may hold values from 1024 to 4096, as said below
- owners: int32 [2], replicated, may hold values from 0 to 63, as said below
- span_q: bfloat16 [2, 2048, 64, 128], P(None, ('tensor', 'section')), may hold values from -22 to 22
- span_k: bfloat16 [2, 2048, 8, 128], P(None, ('tensor', 'section')), may hold values from -6 to 6
- span_v: bfloat16 [2, 2048, 8, 128], P(None, ('tensor', 'section')), may hold values from -6 to 6
- prompt_keys: bfloat16 [2, 4096, 8, 128], P(None, 'section', 'tensor'), may hold values from -6 to 6
- prompt_values: bfloat16 [2, 4096, 8, 128], P(None, 'section', 'tensor'), may hold values from -6 to 6
- res_lengths: int32 [256], P('section'), may hold values from 1 to 1024, as said below
- res_keys: bfloat16 [256, 1024, 8, 128], P('section', None, 'tensor'), may hold values from -6 to 6
- res_values: bfloat16 [256, 1024, 8, 128], P('section', None, 'tensor'), may hold values from -6 to 6
- dec_q: bfloat16 [256, 4, 64, 128], P('section', None, 'tensor'), may hold values from -22 to 22
- dec_k: bfloat16 [256, 4, 8, 128], P('section', None, 'tensor'), may hold values from -6 to 6
- dec_v: bfloat16 [256, 4, 8, 128], P('section', None, 'tensor'), may hold values from -6 to 6
- hand_q: bfloat16 [64, 4, 64, 128], P('section', None, 'tensor'), may hold values from -22 to 22
- hand_k: bfloat16 [64, 4, 8, 128], P('section', None, 'tensor'), may hold values from -6 to 6
- hand_v: bfloat16 [64, 4, 8, 128], P('section', None, 'tensor'), may hold values from -6 to 6
Outputs:
- prefill_out: bfloat16 [2, 2048, 64, 128], P(None, ('tensor', 'section'))
- res_out: bfloat16 [256, 4, 64, 128], P('section', None, 'tensor')
- hand_out: bfloat16 [64, 4, 64, 128], P('section', None, 'tensor')
Inputs may be any that keep to these rules, and one draw needn't show every extreme that they name: `prompt_lengths`: one prompt has exactly 4096 cached positions. The 2 owners are different slots, and one prompt is handed to slot 63. `res_lengths`: some decode row has exactly 1024 cached positions.
All inputs are finite; a program needn't handle non-finite values.
Results may differ from a plain program's by a relative error of at most 0.013.
Values may be sent and summed in bfloat16 or wider, within the bound.
A program may use at most 128 MiB of HBM per device.

v0:
```python
import jax
import jax.numpy as jnp
from jax import lax
from jax.sharding import PartitionSpec as P


def key_layout(first_row, row_count, shard_rows, prompt_rows, block_len, section_count):
    global_row = first_row + jnp.arange(row_count, dtype=jnp.int32)
    source = global_row // shard_rows
    local_row = global_row % shard_rows
    in_prompt = local_row < prompt_rows
    prompt_pos = source * prompt_rows + local_row
    inner_row = jnp.maximum(local_row - prompt_rows, 0)
    span_pos = (inner_row // block_len * section_count + source) * block_len + inner_row % block_len
    return (in_prompt, prompt_pos, span_pos)


def softmax_block(queries, keys_block, values_block, valid_keys, running):
    run_top, run_sum, run_mixed = running
    score_scale = queries.shape[-1] ** (-0.5)
    scores = (
        jnp.einsum("sqhgd,skhd->sqhgk", queries, keys_block, preferred_element_type=jnp.float32)
        * score_scale
    )
    key_mask = valid_keys[:, :, None, None, :]
    scores = jnp.where(key_mask, scores, -1e30)
    new_top = jnp.maximum(run_top, jnp.max(scores, axis=-1))
    rescale = jnp.exp(run_top - new_top)
    weights = jnp.where(key_mask, jnp.exp(scores - new_top[..., None]), 0.0)
    run_sum = run_sum * rescale + jnp.sum(weights, axis=-1)
    update = jnp.einsum(
        "sqhgk,skhd->sqhgd",
        weights.astype(jnp.bfloat16),
        values_block,
        preferred_element_type=jnp.float32,
    )
    run_mixed = run_mixed * rescale[..., None] + update
    return (new_top, run_sum, run_mixed)


def empty_state(lead_shape, head_dim):
    return (
        jnp.full(lead_shape, -1e30, jnp.float32),
        jnp.zeros(lead_shape, jnp.float32),
        jnp.zeros(lead_shape + (head_dim,), jnp.float32),
    )


def finish(running, heads_local):
    run_top, run_sum, run_mixed = running
    normed = (run_mixed / run_sum[..., None]).astype(jnp.bfloat16)
    return normed.reshape(normed.shape[:2] + (heads_local, normed.shape[-1]))


def on_device(
    prompt_lengths,
    owners,
    span_q,
    span_k,
    span_v,
    prompt_keys,
    prompt_values,
    res_lengths,
    res_keys,
    res_values,
    dec_q,
    dec_k,
    dec_v,
    hand_q,
    hand_k,
    hand_v,
):
    section_count = lax.axis_size("section")
    section_index = lax.axis_index("section")
    seq_count = span_q.shape[0]
    block_len = span_q.shape[1]
    head_dim = span_q.shape[3]
    local_q, local_k, local_v = (
        lax.all_to_all(span_q, "tensor", split_axis=2, concat_axis=1, tiled=True),
        lax.all_to_all(span_k, "tensor", split_axis=2, concat_axis=1, tiled=True),
        lax.all_to_all(span_v, "tensor", split_axis=2, concat_axis=1, tiled=True),
    )
    span_rows = local_q.shape[1]
    heads_local = local_q.shape[2]
    kv_local = local_k.shape[2]
    group_size = heads_local // kv_local
    prompt_rows = prompt_keys.shape[1]
    shard_rows = prompt_rows + span_rows
    whole_rows = section_count * shard_rows
    keys_here = jnp.concatenate([prompt_keys, local_k], axis=1)
    values_here = jnp.concatenate([prompt_values, local_v], axis=1)
    query_rows = jnp.arange(span_rows, dtype=jnp.int32)
    query_pos = (
        query_rows // block_len * section_count + section_index
    ) * block_len + query_rows % block_len
    queries = local_q.reshape(seq_count, span_rows, kv_local, group_size, head_dim)
    owned_mask = (owners == section_index).astype(jnp.int32)
    owned_seq = jnp.sum(owned_mask * jnp.arange(seq_count, dtype=jnp.int32))
    owns_any = jnp.sum(owned_mask) > 0
    step_count = hand_q.shape[1]
    step_order = jnp.arange(step_count, dtype=jnp.int32)
    step_valid = step_order[None, :] <= step_order[:, None]
    block_rows = shard_rows * max(1, 2048 // shard_rows)
    prefill_start = empty_state((seq_count, span_rows, kv_local, group_size), head_dim)
    carry_start = (prefill_start,)
    running = carry_start[0]
    piece_keys = lax.all_gather(keys_here, "section", axis=1, tiled=True)
    piece_values = lax.all_gather(values_here, "section", axis=1, tiled=True)
    first_row = jnp.int32(0)
    row_total = piece_keys.shape[1]
    for offset in range(0, row_total, block_rows):
        size_here = min(block_rows, row_total - offset)
        in_prompt, prompt_pos, span_pos = key_layout(
            first_row + offset, size_here, shard_rows, prompt_rows, block_len, section_count
        )
        early_ok = prompt_pos[None, None, :] < prompt_lengths[:, None, None]
        causal_ok = span_pos[None, None, :] <= query_pos[None, :, None]
        valid_keys = jnp.where(in_prompt[None, None, :], early_ok, causal_ok)
        running = softmax_block(
            queries,
            piece_keys[:, offset : offset + size_here],
            piece_values[:, offset : offset + size_here],
            valid_keys,
            running,
        )
    prefill_local = finish(running, heads_local)
    prefill_out = lax.all_to_all(prefill_local, "tensor", split_axis=1, concat_axis=2, tiled=True)
    hand_queries = hand_q.reshape(1, step_count, kv_local, group_size, head_dim)
    own_limit = lax.dynamic_index_in_dim(prompt_lengths, owned_seq, 0, False)
    whole_keys, whole_values = (
        lax.all_gather(keys_here, "section", axis=1, tiled=True),
        lax.all_gather(values_here, "section", axis=1, tiled=True),
    )
    held_keys = lax.dynamic_index_in_dim(whole_keys, owned_seq, 0, False)
    held_values = lax.dynamic_index_in_dim(whole_values, owned_seq, 0, False)
    in_prompt, prompt_pos, span_pos = key_layout(
        0, whole_rows, shard_rows, prompt_rows, block_len, section_count
    )
    held_valid = jnp.logical_or(jnp.logical_not(in_prompt), prompt_pos < own_limit)
    held_valid = jnp.broadcast_to(held_valid[None, None, :], (1, step_count, whole_rows))
    running = softmax_block(
        hand_queries,
        held_keys[None],
        held_values[None],
        held_valid,
        empty_state((1, step_count, kv_local, group_size), head_dim),
    )
    running = softmax_block(hand_queries, hand_k, hand_v, step_valid[None], running)
    handed_local = finish(running, heads_local)
    hand_out = jnp.where(owns_any, handed_local, jnp.zeros_like(handed_local))
    res_count = res_keys.shape[0]
    res_cache = res_keys.shape[1]
    res_queries = dec_q.reshape(res_count, step_count, kv_local, group_size, head_dim)
    cache_ok = jnp.arange(res_cache, dtype=jnp.int32)[None, :] < res_lengths[:, None]
    cache_valid = jnp.broadcast_to(cache_ok[:, None, :], (res_count, step_count, res_cache))
    running = softmax_block(
        res_queries,
        res_keys,
        res_values,
        cache_valid,
        empty_state((res_count, step_count, kv_local, group_size), head_dim),
    )
    running = softmax_block(
        res_queries,
        dec_k,
        dec_v,
        jnp.broadcast_to(step_valid[None], (res_count, step_count, step_count)),
        running,
    )
    res_out = finish(running, heads_local)
    return (prefill_out, res_out, hand_out)


def solution(mesh):
    in_specs = (
        P(),
        P(),
        P(None, ("tensor", "section"), None, None),
        P(None, ("tensor", "section"), None, None),
        P(None, ("tensor", "section"), None, None),
        P(None, "section", "tensor", None),
        P(None, "section", "tensor", None),
        P("section"),
        P("section", None, "tensor", None),
        P("section", None, "tensor", None),
        P("section", None, "tensor", None),
        P("section", None, "tensor", None),
        P("section", None, "tensor", None),
        P("section", None, "tensor", None),
        P("section", None, "tensor", None),
        P("section", None, "tensor", None),
    )
    out_specs = (
        P(None, ("tensor", "section"), None, None),
        P("section", None, "tensor", None),
        P("section", None, "tensor", None),
    )
    return jax.shard_map(
        on_device, mesh=mesh, in_specs=in_specs, out_specs=out_specs, check_vma=False
    )
```

profile of v0, /device:TPU:1, one launch (start us, length us, event | category | flops | bytes accessed | tf_op | source)
XLA Modules:
  0.0 802.6 jit_solution(17571216327780364715)
XLA Ops:
  7.2 1.5 copy.53
  8.7 10.1 %all-to-all-start = ((bf16[2,8,8,128]{3,1,0,2:T(8,128)(2,1)}), bf16[2,8,8,128]{3,1,0,2:T(8,128)(2,1)S(1)}, u32[]{:S(2)}, u32[]{:S(2)}) async-start(bf16[2,8,8,128]{3,1,0,2:T(8,128)(2,1)} %copy.53), calls=%async_computation | async-start | bytes 65536 | tf_op jit(solution)/shard_map/all_to_all | solution.py:80
  18.8 0.9 copy.55
  19.7 6.2 all-to-all-done
  26.6 1.4 copy.58
  27.9 4.0 all-to-all-start.2
  31.9 0.8 copy.60
  32.8 6.2 all-to-all-done.2
  39.7 1.8 copy.56
  41.5 4.2 all-to-all-start.1
  45.7 1.3 fusion.218
  49.5 1.3 fusion.244
  50.8 2.5 fusion.243
  59.0 298.0 %all-gather.3.cloned.1.call-done = bf16[2,6144,2,128]{3,1,2,0:T(8,128)(2,1)} async-done(((bf16[2,96,2,128]{3,1,2,0:T(8,128)(2,1)}), bf16[2,6144,2,128]{3,1,2,0:T(8,128)(2,1)}) %all-gather.3.cloned.1.call-update) | async-done | bytes 6291472 | tf_op jit(solution)/shard_map/all_gather | solution.py:107
  356.9 1.4 fusion.242
  358.3 3.2 fusion.2
  361.6 1.5 fusion.1
  363.1 1.5 fusion
  365.0 2.4 fusion.6
  367.5 2.4 fusion.10
  369.9 2.4 fusion.8
  372.3 351.9 %all-gather.5.cloned.1.call-done = bf16[2,6144,2,128]{3,1,2,0:T(8,128)(2,1)} async-done(((bf16[2,96,2,128]{3,1,2,0:T(8,128)(2,1)}), bf16[2,6144,2,128]{3,1,2,0:T(8,128)(2,1)}) %all-gather.5.cloned.1.call-update) | async-done | bytes 6291472 | tf_op jit(solution)/shard_map/all_gather | solution.py:108
  724.2 5.8 fusion.72
  730.6 1.8 copy-done.8
  732.4 2.3 fusion.66
  734.7 1.0 copy-done.2
  735.8 2.3 fusion.60
  738.5 0.8 copy.61
  739.3 46.7 %all-to-all-start.3 = ((bf16[2,32,16,128]{3,2,0,1:T(8,128)(2,1)}), bf16[2,32,16,128]{3,2,0,1:T(8,128)(2,1)S(1)}, u32[]{:S(2)}, u32[]{:S(2)}) async-start(bf16[2,32,16,128]{3,2,0,1:T(8,128)(2,1)} %copy.61), calls=%async_computation.3 | async-start | bytes 524288 | tf_op jit(solution)/shard_map/all_to_all | solution.py:127
  786.0 3.1 fusion.245
  789.9 2.6 fusion.114
  793.1 1.9 all-to-all-done.3
  (79 shorter events, 10.7 us)
Async XLA Ops:
  7.2 46.9 %copy-start = (bf16[4,1024,2,128]{3,2,1,0:T(2,128)(2,1)S(1)}, bf16[4,1024,2,128]{3,2,1,0:T(2,128)(2,1)}, u32[]{:S(2)}) copy-start(bf16[4,1024,2,128]{3,2,1,0:T(2,128)(2,1)} %param.25) | copy-start | bytes 6291460
  7.2 46.6 %copy-start.6 = (bf16[4,4,2,128]{3,2,1,0:T(2,128)(2,1)S(1)}, bf16[4,4,2,128]{3,2,1,0:T(2,128)(2,1)}, u32[]{:S(2)}) copy-start(bf16[4,4,2,128]{3,2,1,0:T(2,128)(2,1)} %param.28) | copy-start | bytes 24580
  8.7 47.2 %copy-start.7 = (s32[2]{0:T(128)S(1)}, s32[2]{0:T(128)}, u32[]{:S(2)}) copy-start(s32[2]{0:T(128)} %param.16) | copy-start | bytes 28
  8.7 17.2 %all-to-all-start = ((bf16[2,8,8,128]{3,1,0,2:T(8,128)(2,1)}), bf16[2,8,8,128]{3,1,0,2:T(8,128)(2,1)S(1)}, u32[]{:S(2)}, u32[]{:S(2)}) async-start(bf16[2,8,8,128]{3,1,0,2:T(8,128)(2,1)} %copy.53), calls=%async_computation | async-start | bytes 65536 | tf_op jit(solution)/shard_map/all_to_all | solution.py:80
  18.8 38.8 %copy-start.9 = (bf16[1,4,16,128]{3,2,1,0:T(8,128)(2,1)S(1)}, bf16[1,4,16,128]{3,2,1,0:T(8,128)(2,1)}, u32[]{:S(2)}) copy-start(bf16[1,4,16,128]{3,2,1,0:T(8,128)(2,1)} %param.29) | copy-start | bytes 49156
  18.8 38.8 %copy-start.10 = (bf16[1,4,2,128]{3,2,1,0:T(2,128)(2,1)S(1)}, bf16[1,4,2,128]{3,2,1,0:T(2,128)(2,1)}, u32[]{:S(2)}) copy-start(bf16[1,4,2,128]{3,2,1,0:T(2,128)(2,1)} %param.30) | copy-start | bytes 6148
  18.8 338.1 %all-gather.3.cloned.1.call-start = ((), (), s32[]{:S(2)}) async-start(), calls=%async_computation.4 | async-start | bytes 6389760 | tf_op jit(solution)/shard_map/all_gather | solution.py:107
  27.9 11.1 %all-to-all-start.2 = ((bf16[2,8,8,128]{3,1,0,2:T(8,128)(2,1)}), bf16[2,8,8,128]{3,1,0,2:T(8,128)(2,1)S(1)}, u32[]{:S(2)}, u32[]{:S(2)}) async-start(bf16[2,8,8,128]{3,1,0,2:T(8,128)(2,1)} %copy.58), calls=%async_computation.2 | async-start | bytes 65536 | tf_op jit(solution)/shard_map/all_to_all | solution.py:81
  31.9 692.3 %all-gather.5.cloned.1.call-start = ((), (), s32[]{:S(2)}) async-start(), calls=%async_computation.5 | async-start | bytes 6389760 | tf_op jit(solution)/shard_map/all_gather | solution.py:108
  41.5 17.4 %all-to-all-start.1 = ((bf16[2,8,64,128]{3,1,0,2:T(8,128)(2,1)}), bf16[2,8,64,128]{3,1,0,2:T(8,128)(2,1)S(1)}, u32[]{:S(2)}, u32[]{:S(2)}) async-start(bf16[2,8,64,128]{3,1,0,2:T(8,128)(2,1)} %copy.56), calls=%async_computation.1 | async-start | bytes 524288 | tf_op jit(solution)/shard_map/all_to_all | solution.py:79
  356.9 4.7 slice-start
  358.3 3.3 slice-start.1
  361.6 5.9 copy-start.1
  363.1 6.8 copy-start.3
  364.6 5.3 copy-start.5
  724.2 6.4 copy-start.4
  724.2 8.2 %copy-start.8 = (bf16[2,6144,2,128]{3,1,2,0:T(8,128)(2,1)S(1)}, bf16[2,6144,2,128]{3,1,2,0:T(8,128)(2,1)}, u32[]{:S(2)}) copy-start(bf16[2,6144,2,128]{3,1,2,0:T(8,128)(2,1)} %all-gather.5.cloned.1.call-done) | copy-start | bytes 18874372
  732.4 3.4 copy-start.2
  738.1 51.6 %copy-start.11 = (bf16[1,4,2,128]{3,2,1,0:T(2,128)(2,1)S(1)}, bf16[1,4,2,128]{3,2,1,0:T(2,128)(2,1)}, u32[]{:S(2)}) copy-start(bf16[1,4,2,128]{3,2,1,0:T(2,128)(2,1)} %param.31) | copy-start | bytes 6148
  739.3 55.8 %all-to-all-start.3 = ((bf16[2,32,16,128]{3,2,0,1:T(8,128)(2,1)}), bf16[2,32,16,128]{3,2,0,1:T(8,128)(2,1)S(1)}, u32[]{:S(2)}, u32[]{:S(2)}) async-start(bf16[2,32,16,128]{3,2,0,1:T(8,128)(2,1)} %copy.61), calls=%async_computation.3 | async-start | bytes 524288 | tf_op jit(solution)/shard_map/all_to_all | solution.py:127
Sparse Core Ops, SparseCore 0:
  26.7 330.2 all-gather.2
  358.7 365.4 all-gather.4
where the time goes:
time: 803 us
  waiting for transfers between devices  665 us (83%)
  starting transfers between devices  65 us (8%)
  matrix products  29.1 us (4%)
  between operations  16.7 us (2%)
  other arithmetic  13.6 us (2%)
  local copies, waits for them, and re-layouts  13.4 us (2%)
    all_gather x1, waiting for transfers between devices, on_device(): piece_values = lax.all_gather(values_here, 'section', axis=1, tiled=True)  352 us
    all_gather x1, waiting for transfers between devices, on_device(): piece_keys = lax.all_gather(keys_here, 'section', axis=1, tiled=True)  298 us
    all_to_all x1, starting transfers between devices, on_device(): lax.all_to_all(prefill_local, 'tensor', split_axis=1, concat_axis=2, tile...  46.7 us
  transfers between devices with their start and end apart: 6, of which 6 were waited for; matrix products, arithmetic and copies ran while one was open for 5% of the time, Pallas kernels for 0%

commit v1 on v0

v1 whole, which is shorter than its diff:
```python
import jax
import jax.numpy as jnp
from jax import lax
from jax.experimental import pallas as pl
from jax.experimental.pallas import tpu as pltpu
from jax.sharding import PartitionSpec as P

MESH = pl.DeviceIdType.MESH
F32 = jnp.float32
BF16 = jnp.bfloat16
SCALE = 128 ** -0.5 * 1.4426950408889634
LOW = -1e30
ROWS = 512


def device_at(x, y, z, c):
    return ((z // 4) * 2 + c, y * 16 + x * 4 + z % 4)


def dot_t(a, b):
    return lax.dot_general(a, b, (((1,), (1,)), ((), ())), preferred_element_type=F32)


def dot(a, b):
    return jnp.dot(a, b, preferred_element_type=F32)


def kernel(
    plen, owners, rlen, span_q, span_k, span_v, prompt_k, prompt_v, res_k, res_v,
    dec_q, dec_k, dec_v, hand_q, hand_k, hand_v,
    out_p, out_r, out_h,
    in_q, in_k, in_v, in_pk, in_pv, in_rk, in_rv,
    wide, stq, rcq, stp, rcp, kv, top, total, mixed, dmat, sto, rco, sth, rch,
    outbuf, resbuf, dkpad, dvpad,
    sem_in, sem_rk, sem_rv, sem_out,
    q_send, q_recv, p_send, p_recv, ring_send, ring_recv, sib_send, sib_recv,
    o_send, o_recv, h_send, h_recv,
):
    t = lax.axis_index("tensor")
    s = lax.axis_index("section")
    zh, c = t // 2, t % 2
    x, y, zl = (s // 4) % 4, s // 16, s % 4
    z = zh * 4 + zl
    j = s // 4
    seq, half = y // 2, y % 2

    def copy_in(a, b, sem):
        cp = pltpu.make_async_copy(a, b, sem)
        cp.start()
        return cp

    cps_p = [copy_in(prompt_k, in_pk, sem_in.at[0]), copy_in(prompt_v, in_pv, sem_in.at[1])]
    cps_s = [
        copy_in(span_k, in_k, sem_in.at[2]),
        copy_in(span_v, in_v, sem_in.at[3]),
        copy_in(span_q, in_q, sem_in.at[4]),
    ]
    cps_k = [copy_in(res_k.at[r], in_rk.at[r], sem_rk.at[r]) for r in range(4)]
    cps_v = [copy_in(res_v.at[r], in_rv.at[r], sem_rv.at[r]) for r in range(4)]

    def column(jj):
        return device_at(jj % 4, jj // 4, z, c)

    up = device_at(x, y, (z + 1) % 8, c)
    down = device_at(x, y, (z + 7) % 8, c)
    sib = device_at(x, y, z, 1 - c)

    p_dest = []
    for sq in range(2):
        for hl in range(2):
            xd, yd, cd = 2 * c + hl, 2 * sq + zh, x % 2
            zd = (z + 4 * (x // 2)) % 8
            same = (xd == x) & (yd == y) & (x // 2 == 0) & (cd == c)
            p_dest.append((device_at(xd, yd, zd, cd), same))
    p_src = []
    away = jnp.where(zh == half, 0, 1)
    for ys in range(4):
        xs, cs = 2 * away + c, x // 2
        zs = (z + 4 * away) % 8
        same = (xs == x) & (ys == y) & (away == 0) & (cs == c)
        p_src.append((device_at(xs, ys, zs, cs), same))
    h_dest = []
    for xd in range(4):
        yd, zd, cd = 2 * zh + c, 4 * half + zl, x // 2
        same = (xd == x) & (yd == y) & (zd == z) & (cd == c)
        h_dest.append((device_at(xd, yd, zd, cd), same))
    h_src = []
    for sq in range(2):
        for hl in range(2):
            xs, ys, zs, cs = 2 * c + hl, 2 * sq + zh, (y // 2) * 4 + zl, y % 2
            same = (xs == x) & (ys == y) & (zs == z) & (cs == c)
            h_src.append((device_at(xs, ys, zs, cs), same))

    bar = pltpu.get_barrier_semaphore()

    def greet(where):
        pl.semaphore_signal(bar, inc=1, device_id=where, device_id_type=MESH)

    def greet_column(d, carry):
        greet(column((j + d) % 16))
        return carry

    lax.fori_loop(1, 16, greet_column, 0)
    for where in (up, down, sib):
        greet(where)
    for where, same in p_src + h_src:

        @pl.when(jnp.logical_not(same))
        def _():
            greet(where)

    expect = 18
    for _, same in p_dest + h_dest:
        expect = expect + jnp.where(same, 0, 1)

    hq = hand_q[...].astype(F32)
    hkv = jnp.concatenate([hand_k[...].astype(F32), hand_v[...].astype(F32)], axis=0)
    for cp in cps_p:
        cp.wait()
    for sq in range(2):
        wide[2 * sq] = in_pk[sq].astype(F32)
        wide[2 * sq + 1] = in_pv[sq].astype(F32)
    for sq in range(2):
        mine = jnp.where(owners[sq] == s, 1.0, 0.0)
        for hl in range(2):
            k = 2 * sq + hl
            stp[k, 0:64, :] = wide[2 * sq, pl.ds(hl, 64, stride=2), :].astype(BF16)
            stp[k, 64:128, :] = wide[2 * sq + 1, pl.ds(hl, 64, stride=2), :].astype(BF16)
            block = jnp.concatenate([hq[:, 8 * hl : 8 * hl + 8, :].reshape(32, 128), hkv], axis=0)
            stp[k, 128:176, :] = (block * mine).astype(BF16)

    pl.semaphore_wait(bar, expect)

    for k, (where, same) in enumerate(p_dest):

        @pl.when(jnp.logical_not(same))
        def _():
            pltpu.make_async_remote_copy(
                stp.at[k], rcp.at[y], p_send.at[k], p_recv, device_id=where, device_id_type=MESH
            ).start()

        @pl.when(same)
        def _():
            pltpu.make_async_copy(stp.at[k], rcp.at[y], p_recv).start()

    for cp in cps_s:
        cp.wait()
    for sq in range(2):
        wide[sq, 0:64, :] = in_k[sq].astype(F32).reshape(64, 128)
        wide[sq, 64:128, :] = in_v[sq].astype(F32).reshape(64, 128)
    for sq in range(2):
        for hh in range(4):
            two = in_q[sq, :, 16 * hh : 16 * hh + 16, :].astype(F32)
            for e in range(2):
                h = 2 * hh + e
                stq[8 * sq + h, 0:64, :] = two[:, 8 * e : 8 * e + 8, :].reshape(64, 128).astype(BF16)
                stq[8 * sq + h, 64:80, :] = jnp.concatenate(
                    [wide[sq, pl.ds(h, 8, stride=8), :], wide[sq, pl.ds(64 + h, 8, stride=8), :]], axis=0
                ).astype(BF16)

    def send_q(d, carry):
        jj = (j + d) % 16
        pltpu.make_async_remote_copy(
            stq.at[jj], rcq.at[j], q_send, q_recv, device_id=column(jj), device_id_type=MESH
        ).start()
        return carry

    lax.fori_loop(1, 16, send_q, 0)
    pltpu.make_async_copy(stq.at[j], rcq.at[j], q_recv).start()

    row = lax.broadcasted_iota(jnp.int32, (1024, 128), 0)
    lane = lax.broadcasted_iota(jnp.int32, (1024, 128), 1)
    dmat[...] = (
        32 * (row // 64) + (row % 64) // 8 - 32 * (lane // 8) - lane % 8
    ).astype(F32)
    top[...] = jnp.full((1024, 128), LOW, F32)
    total[...] = jnp.zeros((1024, 128), F32)
    mixed[...] = jnp.zeros((1024, 128), F32)

    dkpad[...] = jnp.zeros((128, 128), BF16)
    dvpad[...] = jnp.zeros((128, 128), BF16)
    dkpad[0:32, :] = dec_k[...]
    dvpad[0:32, :] = dec_v[...]
    col = lax.broadcasted_iota(jnp.int32, (8, 2048), 1)
    row64 = lax.broadcasted_iota(jnp.int32, (64, 128), 0)
    lane64 = lax.broadcasted_iota(jnp.int32, (64, 128), 1)
    own_ok = (lane64 % 2 == (row64 // 8) % 2) & ((lane64 % 8) // 2 <= row64 // 16)
    for r in range(4):
        cps_k[r].wait()
        qr = dec_q[r]
        sc = dot_t(qr, in_rk[r])
        inside = col // 2 < rlen[r]
        b0 = jnp.where(inside & (col % 2 == 0), 0.0, LOW)
        b1 = jnp.where(inside & (col % 2 == 1), 0.0, LOW)
        both = jnp.concatenate([b0, b1], axis=0)
        sc = sc + jnp.concatenate([both] * 4, axis=0)
        so = jnp.where(own_ok & (lane64 // 8 == r), dot_t(qr, dkpad[...]), LOW)
        mx = jnp.maximum(jnp.max(sc, axis=1, keepdims=True), jnp.max(so, axis=1, keepdims=True))
        ps = jnp.exp2((sc - mx) * SCALE)
        po = jnp.exp2((so - mx) * SCALE)
        den = jnp.sum(ps, axis=1, keepdims=True) + jnp.sum(po, axis=1, keepdims=True)
        cps_v[r].wait()
        num = dot(ps.astype(BF16), in_rv[r]) + dot(po.astype(BF16), dvpad[...])
        resbuf[r] = (num / den).astype(BF16)
    cp_res = pltpu.make_async_copy(resbuf, out_r, sem_out.at[1])
    cp_res.start()

    def recv(ref, sem):
        pltpu.make_async_remote_copy(ref, ref, h_send.at[0], sem, device_id=sib, device_id_type=MESH).wait_recv()

    recv(rcp, p_recv)
    handed = rcp[0, 128:176, :].astype(F32)
    for ys in range(4):
        kv[0, c, 64 * ys : 64 * ys + 64, :] = rcp[ys, 0:64, :]
        kv[0, c, 432 + 64 * ys : 496 + 64 * ys, :] = rcp[ys, 64:128, :]
        if ys:
            handed = handed + rcp[ys, 128:176, :].astype(F32)
    kv[0, c, 384:432, :] = handed.astype(BF16)
    recv(rcq, q_recv)
    new = rcq[:, 64:80, :].astype(F32)
    kv[0, c, 256:384, :] = new[:, 0:8, :].reshape(128, 128).astype(BF16)
    kv[0, c, 688:816, :] = new[:, 8:16, :].reshape(128, 128).astype(BF16)

    parts = (pl.ds(0, 432), pl.ds(432, 384))

    def hop(src, dst, part, where, lane_index):
        pltpu.make_async_remote_copy(
            kv.at[src, c, parts[part]], kv.at[dst, c, parts[part]],
            ring_send.at[lane_index], ring_recv.at[dst, part], device_id=where, device_id_type=MESH,
        ).start()

    def share(slot, part):
        pltpu.make_async_remote_copy(
            kv.at[slot, c, parts[part]], kv.at[slot, c, parts[part]],
            sib_send, sib_recv.at[slot, part], device_id=sib, device_id_type=MESH,
        ).start()

    def arrive(slot, part):
        recv(kv.at[slot, c, parts[part]], ring_recv.at[slot, part])

    def shared(slot):
        for part in (0, 1):
            recv(kv.at[slot, 1 - c, parts[part]], sib_recv.at[slot, part])

    plen_here = plen[seq]
    lane1 = lax.broadcasted_iota(jnp.int32, (1, 128), 1)
    lane_pos = 1024 * (lane1 // 64) + lane1 % 64
    z_of = [z, (z + 7) % 8, (z + 1) % 8, (z + 6) % 8, (z + 2) % 8, (z + 5) % 8, (z + 3) % 8, (z + 4) % 8]

    def prompt_bias(slot, cc):
        zz = z_of[slot]
        off = 256 * (cc + 2 * jnp.where(zz // 4 == half, 0, 1)) + 64 * (zz % 4)
        return [jnp.where(lane_pos + (off + 2048 * e) < plen_here, 0.0, LOW) for e in range(2)]

    def process(slots):
        blocks = [(slot, cc) for slot in slots for cc in range(2)]
        bias = [prompt_bias(slot, cc) for slot, cc in blocks]
        limit = [
            (512 * (2 * (z_of[slot] // 4) + cc - t) + 8 * (z_of[slot] % 4 - zl)).astype(F32)
            for slot, cc in blocks
        ]

        def tile(n):
            rs = pl.ds(n * ROWS, ROWS)
            q = rcq[n * (ROWS // 64) : (n + 1) * (ROWS // 64), 0:64, :].reshape(ROWS, 128)
            keys = jnp.concatenate([kv[slot, cc, 0:384, :] for slot, cc in blocks], axis=0)
            values = jnp.concatenate([kv[slot, cc, 432:816, :] for slot, cc in blocks], axis=0)
            sc = dot_t(q, keys)
            ss = []
            for i in range(len(blocks)):
                ss.append(sc[:, 384 * i : 384 * i + 128] + bias[i][0])
                ss.append(sc[:, 384 * i + 128 : 384 * i + 256] + bias[i][1])
                ss.append(jnp.where(dmat[rs, :] >= limit[i], sc[:, 384 * i + 256 : 384 * i + 384], LOW))
            mx = ss[0]
            for v in ss[1:]:
                mx = jnp.maximum(mx, v)
            old = top[rs, :]
            now = jnp.maximum(old, jnp.max(mx, axis=1, keepdims=True))
            shrink = jnp.exp2((old - now) * SCALE)
            top[rs, :] = now
            ps = [jnp.exp2((v - now) * SCALE) for v in ss]
            su = ps[0]
            for v in ps[1:]:
                su = su + v
            p = jnp.concatenate([v.astype(BF16) for v in ps], axis=1)
            mixed[rs, :] = mixed[rs, :] * shrink + dot(p, values)
            total[rs, :] = total[rs, :] * shrink + su

        for n in range(1024 // ROWS):
            tile(n)

    for part in (0, 1):
        hop(0, 1, part, up, 0)
        hop(0, 2, part, down, 1)
        share(0, part)
    shared(0)
    process([0])
    for a in (1, 2, 3):
        plus, minus = 2 * a - 1, 2 * a
        for part in (0, 1):
            arrive(plus, part)
            if a < 3:
                hop(plus, plus + 2, part, up, 0)
            elif part == 0:
                hop(plus, 7, part, up, 2)
            arrive(minus, part)
            if a < 3:
                hop(minus, minus + 2, part, down, 1)
            elif part == 1:
                hop(minus, 7, part, down, 3)
            share(plus, part)
            share(minus, part)
        shared(plus)
        shared(minus)
        process([plus, minus])
    for part in (0, 1):
        arrive(7, part)
        share(7, part)
    shared(7)
    process([7])

    sto[...] = (mixed[...] / jnp.sum(total[...], axis=1, keepdims=True)).astype(BF16).reshape(16, 64, 128)

    def send_o(d, carry):
        jj = (j + d) % 16
        pltpu.make_async_remote_copy(
            sto.at[jj], rco.at[j], o_send, o_recv, device_id=column(jj), device_id_type=MESH
        ).start()
        return carry

    lax.fori_loop(1, 16, send_o, 0)
    pltpu.make_async_copy(sto.at[j], rco.at[j], o_recv).start()

    hsum = jnp.zeros((48, 128), F32)
    for slot in range(8):
        for cc in range(2):
            hsum = hsum + kv[slot, cc, 384:432, :].astype(F32)
    qh = hsum[0:32, :].astype(BF16)
    dkpad[...] = jnp.zeros((128, 128), BF16)
    dvpad[...] = jnp.zeros((128, 128), BF16)
    zero8 = jnp.zeros((8, 128), F32)
    dkpad[0:16, :] = jnp.concatenate([hsum[32:40, :], zero8], axis=0).astype(BF16)
    dvpad[0:16, :] = jnp.concatenate([hsum[40:48, :], zero8], axis=0).astype(BF16)
    row32 = lax.broadcasted_iota(jnp.int32, (32, 128), 0)
    lane32 = lax.broadcasted_iota(jnp.int32, (32, 128), 1)
    ok = (lane32 < 8) & (lane32 % 2 == x % 2) & (lane32 // 2 <= row32 // 8)
    so = jnp.where(ok, dot_t(qh, dkpad[...]), LOW)
    ss = []
    for slot in range(8):
        for cc in range(2):
            sc = dot_t(qh, kv[slot, cc, 0:384, :])
            bias = prompt_bias(slot, cc)
            ss.append([sc[:, 0:128] + bias[0], sc[:, 128:256] + bias[1], sc[:, 256:384]])
    mx = so
    for three in ss:
        for v in three:
            mx = jnp.maximum(mx, v)
    mx = jnp.max(mx, axis=1, keepdims=True)
    po = jnp.exp2((so - mx) * SCALE)
    su = po
    num = dot(po.astype(BF16), dvpad[...])
    for i, three in enumerate(ss):
        ps = [jnp.exp2((v - mx) * SCALE) for v in three]
        su = su + ps[0] + ps[1] + ps[2]
        p = jnp.concatenate([v.astype(BF16) for v in ps], axis=1)
        num = num + dot(p, kv[i // 2, i % 2, 432:816, :])
    sth[...] = (num / jnp.sum(su, axis=1, keepdims=True)).astype(BF16)
    slot_h = seq * 2 + x % 2
    for k, (where, same) in enumerate(h_dest):

        @pl.when(jnp.logical_not(same))
        def _():
            pltpu.make_async_remote_copy(
                sth, rch.at[slot_h], h_send.at[k], h_recv, device_id=where, device_id_type=MESH
            ).start()

        @pl.when(same)
        def _():
            pltpu.make_async_copy(sth, rch.at[slot_h], h_recv).start()

    recv(rco, o_recv)
    for sq in range(2):
        for hh in range(4):
            a = rco[8 * sq + 2 * hh].astype(F32).reshape(8, 8, 128)
            b = rco[8 * sq + 2 * hh + 1].astype(F32).reshape(8, 8, 128)
            outbuf[sq, :, 16 * hh : 16 * hh + 16, :] = jnp.concatenate([a, b], axis=1).astype(BF16)
    cp_out = pltpu.make_async_copy(outbuf, out_p, sem_out.at[0])
    cp_out.start()
    recv(rch, h_recv)
    heads = []
    for hl in range(2):
        acc = jnp.zeros((32, 128), F32)
        for sq in range(2):
            mine = jnp.where(owners[sq] == s, 1.0, 0.0)
            acc = acc + rch[2 * sq + hl].astype(F32) * mine
        heads.append(acc.reshape(4, 8, 128))
    out_h[...] = jnp.concatenate(heads, axis=1).astype(BF16)

    def sent(ref, sem):
        pltpu.make_async_remote_copy(ref, ref, sem, h_recv, device_id=sib, device_id_type=MESH).wait_send()

    for k, (_, same) in enumerate(p_dest):

        @pl.when(jnp.logical_not(same))
        def _():
            sent(stp.at[k], p_send.at[k])

    for k, (_, same) in enumerate(h_dest):

        @pl.when(jnp.logical_not(same))
        def _():
            sent(sth, h_send.at[k])

    sent(stq.at[pl.ds(0, 15)], q_send)
    sent(sto.at[pl.ds(0, 15)], o_send)
    sent(kv.at[pl.ds(0, 3), 0], ring_send.at[0])
    sent(kv.at[pl.ds(0, 3), 0], ring_send.at[1])
    sent(kv.at[0, 0, parts[0]], ring_send.at[2])
    sent(kv.at[0, 0, parts[1]], ring_send.at[3])
    sent(kv.at[pl.ds(0, 8), 0], sib_send)
    cp_out.wait()
    cp_res.wait()


def on_device(
    prompt_lengths, owners, span_q, span_k, span_v, prompt_keys, prompt_values, res_lengths,
    res_keys, res_values, dec_q, dec_k, dec_v, hand_q, hand_k, hand_v,
):
    smem = pl.BlockSpec(memory_space=pltpu.SMEM)
    hbm = pl.BlockSpec(memory_space=pl.ANY)
    vmem = pl.BlockSpec(memory_space=pltpu.VMEM)
    dma = pltpu.SemaphoreType.DMA
    out = pl.pallas_call(
        kernel,
        out_shape=(
            jax.ShapeDtypeStruct((2, 8, 64, 128), BF16),
            jax.ShapeDtypeStruct((4, 64, 128), BF16),
            jax.ShapeDtypeStruct((4, 16, 128), BF16),
        ),
        in_specs=[smem] * 3 + [hbm] * 7 + [vmem] * 6,
        out_specs=(hbm, hbm, vmem),
        scratch_shapes=[
            pltpu.VMEM((2, 8, 64, 128), BF16),
            pltpu.VMEM((2, 8, 8, 128), BF16),
            pltpu.VMEM((2, 8, 8, 128), BF16),
            pltpu.VMEM((2, 128, 128), BF16),
            pltpu.VMEM((2, 128, 128), BF16),
            pltpu.VMEM((4, 2048, 128), BF16),
            pltpu.VMEM((4, 2048, 128), BF16),
            pltpu.VMEM((4, 128, 128), F32),
            pltpu.VMEM((16, 80, 128), BF16),
            pltpu.VMEM((16, 80, 128), BF16),
            pltpu.VMEM((4, 176, 128), BF16),
            pltpu.VMEM((4, 176, 128), BF16),
            pltpu.VMEM((8, 2, 816, 128), BF16),
            pltpu.VMEM((1024, 128), F32),
            pltpu.VMEM((1024, 128), F32),
            pltpu.VMEM((1024, 128), F32),
            pltpu.VMEM((1024, 128), F32),
            pltpu.VMEM((16, 64, 128), BF16),
            pltpu.VMEM((16, 64, 128), BF16),
            pltpu.VMEM((32, 128), BF16),
            pltpu.VMEM((4, 32, 128), BF16),
            pltpu.VMEM((2, 8, 64, 128), BF16),
            pltpu.VMEM((4, 64, 128), BF16),
            pltpu.VMEM((128, 128), BF16),
            pltpu.VMEM((128, 128), BF16),
            dma((5,)), dma((4,)), dma((4,)), dma((2,)),
            dma, dma, dma((4,)), dma, dma((4,)), dma((8, 2)), dma, dma((8, 2)),
            dma, dma, dma((4,)), dma,
        ],
        compiler_params=pltpu.CompilerParams(
            collective_id=0, has_side_effects=True, vmem_limit_bytes=52 << 20
        ),
        name="spanned",
    )(
        prompt_lengths, owners, res_lengths, span_q, span_k, span_v,
        prompt_keys.reshape(2, 128, 128), prompt_values.reshape(2, 128, 128),
        res_keys.reshape(4, 2048, 128), res_values.reshape(4, 2048, 128),
        dec_q.reshape(4, 64, 128), dec_k.reshape(32, 128), dec_v.reshape(32, 128),
        hand_q.reshape(4, 16, 128), hand_k.reshape(8, 128), hand_v.reshape(8, 128),
    )
    prefill_out, res_out, hand_out = out
    return (prefill_out, res_out.reshape(4, 4, 16, 128), hand_out.reshape(1, 4, 16, 128))


def solution(mesh):
    cache = P("section", None, "tensor", None)
    span = P(None, ("tensor", "section"), None, None)
    prompt = P(None, "section", "tensor", None)
    return jax.shard_map(
        on_device,
        mesh=mesh,
        in_specs=(P(), P(), span, span, span, prompt, prompt, P("section")) + (cache,) * 8,
        out_specs=(span, cache, cache),
        check_vma=False,
    )
```

time: 803 us -> 70.4 us (0.09)
  waiting for transfers between devices: 665 us -> 0 us
  starting transfers between devices: 65 us -> 0 us
  Pallas kernels: 0 us -> 56.8 us
  matrix products: 29.1 us -> 0 us
  between operations: 16.7 us -> 0.67 us
  other arithmetic: 13.6 us -> 0 us
    all_gather x2 -> x0, waiting for transfers between devices: 650 us -> none  [the longest x1 352 us: on_device(): piece_values = lax.all_gather(values_here, 'section', axis=1, tiled=True)]
    all_to_all x4 -> x0, starting transfers between devices: 65 us -> none  [the longest x1 46.7 us: on_device(): lax.all_to_all(prefill_local, 'tensor', split_axis=1, concat_axis=2, tile...]
    pallas_call x0 -> x1, Pallas kernels: none -> 56.8 us  [on_device(): pl.pallas_call(kernel, out_shape=(jax.ShapeDtypeStruct((2, 8, 64, 128), B...]
    dot_general x16 -> x0, matrix products: 29.1 us -> none  [the longest x8 14.7 us: softmax_block(): jnp.einsum('sqhgd,skhd->sqhgk', queries, keys_block, preferred_element_ty...]
    all_to_all x4 -> x0, waiting for transfers between devices: 14.9 us -> none  [the longest x1 6.23 us: on_device(): lax.all_to_all(span_v, 'tensor', split_axis=2, concat_axis=1, tiled=True)]
    reduce_sum x9 -> x0, other arithmetic: 9.94 us -> none  [the longest x8 8.65 us: softmax_block(): run_sum = run_sum * rescale + jnp.sum(weights, axis=-1)]
  transfers between devices with their start and end apart: 6 -> 0, of which waited for: 6 -> 0; matrix products, arithmetic and copies ran while one was open for 5% -> 0% of each run, Pallas kernels for 0% -> 0%
where the time goes in v1:
time: 70.4 us; the launch traced here: 69.8 us
  Pallas kernels  56.8 us (81%)
  local copies, waits for them, and re-layouts  12.3 us (17%)
    pallas_call x1, Pallas kernels, on_device(): pl.pallas_call(kernel, out_shape=(jax.ShapeDtypeStruct((2, 8, 64, 128), B...  56.8 us
    unnamed x31, local copies, waits for them, and re-layouts  12.3 us

profile of v1, /device:TPU:1, one launch (start us, length us, event | category | flops | bytes accessed | tf_op | source)
XLA Modules:
  0.0 69.8 jit_solution(1435834949113124591)
XLA Ops:
  0.6 0.0 copy-start
  0.6 0.9 %copy-done = bf16[2,8,64,128]{3,2,1,0:T(8,128)(2,1)S(1)} copy-done((bf16[2,8,64,128]{3,2,1,0:T(8,128)(2,1)S(1)}, bf16[2,8,64,128]{3,2,1,0:T(8,128)(2,1)}, u32[]{:S(2)}) %copy-start) | copy-done | bytes 262168
  1.6 0.0 copy-start.1
  1.6 0.8 %copy-done.1 = bf16[2,64,2,128]{3,2,1,0:T(2,128)(2,1)S(1)} copy-done((bf16[2,64,2,128]{3,2,1,0:T(2,128)(2,1)S(1)}, bf16[2,64,2,128]{3,2,1,0:T(2,128)(2,1)}, u32[]{:S(2)}) %copy-start.1) | copy-done | bytes 65560
  2.4 0.0 copy-start.2
  2.4 0.8 %copy-done.2 = bf16[2,64,2,128]{3,2,1,0:T(2,128)(2,1)S(1)} copy-done((bf16[2,64,2,128]{3,2,1,0:T(2,128)(2,1)S(1)}, bf16[2,64,2,128]{3,2,1,0:T(2,128)(2,1)}, u32[]{:S(2)}) %copy-start.2) | copy-done | bytes 65560
  3.3 0.0 copy-start.3
  3.3 0.8 %copy-done.3 = bf16[4,4,16,128]{3,2,1,0:T(8,128)(2,1)S(1)} copy-done((bf16[4,4,16,128]{3,2,1,0:T(8,128)(2,1)S(1)}, bf16[4,4,16,128]{3,2,1,0:T(8,128)(2,1)}, u32[]{:S(2)}) %copy-start.3) | copy-done | bytes 65560
  4.1 0.0 copy-start.4
  4.1 0.8 %copy-done.4 = bf16[2,8,8,128]{3,2,1,0:T(8,128)(2,1)S(1)} copy-done((bf16[2,8,8,128]{3,2,1,0:T(8,128)(2,1)S(1)}, bf16[2,8,8,128]{3,2,1,0:T(8,128)(2,1)}, u32[]{:S(2)}) %copy-start.4) | copy-done | bytes 32792
  4.9 0.0 copy-start.5
  4.9 0.8 %copy-done.5 = bf16[2,8,8,128]{3,2,1,0:T(8,128)(2,1)S(1)} copy-done((bf16[2,8,8,128]{3,2,1,0:T(8,128)(2,1)S(1)}, bf16[2,8,8,128]{3,2,1,0:T(8,128)(2,1)}, u32[]{:S(2)}) %copy-start.5) | copy-done | bytes 32792
  5.6 0.0 copy-start.6
  5.6 0.7 %copy-done.6 = bf16[1,4,16,128]{3,2,1,0:T(8,128)(2,1)S(1)} copy-done((bf16[1,4,16,128]{3,2,1,0:T(8,128)(2,1)S(1)}, bf16[1,4,16,128]{3,2,1,0:T(8,128)(2,1)}, u32[]{:S(2)}) %copy-start.6) | copy-done | bytes 16408
  6.3 0.0 copy-start.7
  6.3 0.7 copy-done.7
  7.0 0.0 copy-start.8
  7.0 0.7 copy-done.8
  7.7 0.0 copy-start.9
  7.7 0.7 copy-done.9
  8.4 0.0 copy-start.10
  8.4 0.7 copy-done.10
  9.1 0.0 copy-start.11
  9.1 0.7 copy-done.11
  9.8 0.0 copy-start.12
  9.8 0.7 copy-done.12
  10.4 0.0 copy-start.13
  10.4 0.7 copy-done.13
  11.1 56.8 %spanned.1 = (bf16[2,8,64,128]{3,2,1,0:T(8,128)(2,1)S(1)}, bf16[4,64,128]{2,1,0:T(8,128)(2,1)S(1)}, bf16[4,16,128]{2,1,0:T(8,128)(2,1)S(1)}) custom-call(s32[2]{0:T(128)S(1)} %copy-done.11, s32[2]{0:T(128)S(1)} %copy-done.12, s32[4]{0:T(128)S(1)} %copy-done.13, bf16[2,8,64,128]{3,2,1,0:T(8,128)(2,1)S(1)} %copy-done, bf16[2,8,8,128]{3,2,1,0:T(8,128)(2,1)S(1)} %copy-done.4, ...), custom_call_target="tpu_custom_call" | custom-call | tf_op jit(solution)/shard_map/spanned/pallas_call | solution.py:433
  67.8 0.7 %copy.22 = bf16[2,8,64,128]{3,2,1,0:T(8,128)(2,1)} copy(bf16[2,8,64,128]{3,2,1,0:T(8,128)(2,1)S(1)} %get-tuple-element.12) | data formatting | bytes 524288
  68.6 0.6 copy.23
  69.2 0.6 copy.24
Async XLA Ops:
  0.6 1.0 %copy-start = (bf16[2,8,64,128]{3,2,1,0:T(8,128)(2,1)S(1)}, bf16[2,8,64,128]{3,2,1,0:T(8,128)(2,1)}, u32[]{:S(2)}) copy-start(bf16[2,8,64,128]{3,2,1,0:T(8,128)(2,1)} %span_q.1) | copy-start | bytes 786436
  1.6 0.8 %copy-start.1 = (bf16[2,64,2,128]{3,2,1,0:T(2,128)(2,1)S(1)}, bf16[2,64,2,128]{3,2,1,0:T(2,128)(2,1)}, u32[]{:S(2)}) copy-start(bf16[2,64,2,128]{3,2,1,0:T(2,128)(2,1)} %param.21) | copy-start | bytes 196612
  2.4 0.8 %copy-start.2 = (bf16[2,64,2,128]{3,2,1,0:T(2,128)(2,1)S(1)}, bf16[2,64,2,128]{3,2,1,0:T(2,128)(2,1)}, u32[]{:S(2)}) copy-start(bf16[2,64,2,128]{3,2,1,0:T(2,128)(2,1)} %param.22) | copy-start | bytes 196612
  3.3 0.8 %copy-start.3 = (bf16[4,4,16,128]{3,2,1,0:T(8,128)(2,1)S(1)}, bf16[4,4,16,128]{3,2,1,0:T(8,128)(2,1)}, u32[]{:S(2)}) copy-start(bf16[4,4,16,128]{3,2,1,0:T(8,128)(2,1)} %param.26) | copy-start | bytes 196612
  4.1 0.8 %copy-start.4 = (bf16[2,8,8,128]{3,2,1,0:T(8,128)(2,1)S(1)}, bf16[2,8,8,128]{3,2,1,0:T(8,128)(2,1)}, u32[]{:S(2)}) copy-start(bf16[2,8,8,128]{3,2,1,0:T(8,128)(2,1)} %span_k.1) | copy-start | bytes 98308
  4.9 0.8 %copy-start.5 = (bf16[2,8,8,128]{3,2,1,0:T(8,128)(2,1)S(1)}, bf16[2,8,8,128]{3,2,1,0:T(8,128)(2,1)}, u32[]{:S(2)}) copy-start(bf16[2,8,8,128]{3,2,1,0:T(8,128)(2,1)} %span_v.1) | copy-start | bytes 98308
  5.6 0.7 %copy-start.6 = (bf16[1,4,16,128]{3,2,1,0:T(8,128)(2,1)S(1)}, bf16[1,4,16,128]{3,2,1,0:T(8,128)(2,1)}, u32[]{:S(2)}) copy-start(bf16[1,4,16,128]{3,2,1,0:T(8,128)(2,1)} %param.29) | copy-start | bytes 49156
  6.3 0.7 copy-start.7
  7.0 0.7 copy-start.8
  7.7 0.7 copy-start.9
  8.4 0.7 copy-start.10
  9.1 0.7 copy-start.11
  9.8 0.7 copy-start.12
  10.4 0.7 copy-start.13

commit v2 on v1

v2 whole, which is shorter than its diff:
```python
import jax
import jax.numpy as jnp
from jax import lax
from jax.experimental import pallas as pl
from jax.experimental.pallas import tpu as pltpu
from jax.sharding import PartitionSpec as P

MESH = pl.DeviceIdType.MESH
F32 = jnp.float32
BF16 = jnp.bfloat16
SCALE = 128 ** -0.5 * 1.4426950408889634
LOW = -1e30
ROWS = 512


def device_at(x, y, z, c):
    return ((z // 4) * 2 + c, y * 16 + x * 4 + z % 4)


def dot_t(a, b):
    return lax.dot_general(a, b, (((1,), (1,)), ((), ())), preferred_element_type=F32)


def dot(a, b):
    return jnp.dot(a, b, preferred_element_type=F32)


def kernel(
    plen_h, owners_h, rlen_h, span_q, span_k, span_v, prompt_k, prompt_v, res_k, res_v,
    dec_q_h, dec_k_h, dec_v_h, hand_q_h, hand_k_h, hand_v_h,
    rco, out_r, out_h,
    in_q, in_k, in_v, in_pk, in_pv, in_rk, in_rv,
    plen, owners, rlen, dec_q, dec_k, dec_v, hand_q, hand_k, hand_v, hbuf,
    wide, stn, rcn, stq, rcq, stp, rcp, kv, top, total, mixed, dmat, sto, sth, rch,
    resbuf, dkpad, dvpad,
    sem_in, sem_rk, sem_rv, sem_out,
    n_send, n_recv, q_send, q_recv, p_send, p_recv, ring_send, ring_recv, sib_send, sib_recv,
    o_send, o_recv, h_send, h_recv,
):
    t = lax.axis_index("tensor")
    s = lax.axis_index("section")
    zh, c = t // 2, t % 2
    x, y, zl = (s // 4) % 4, s // 16, s % 4
    z = zh * 4 + zl
    j = s // 4
    seq, half = y // 2, y % 2

    def copy_in(a, b, sem):
        cp = pltpu.make_async_copy(a, b, sem)
        cp.start()
        return cp

    def column(jj):
        return device_at(jj % 4, jj // 4, z, c)

    up = device_at(x, y, (z + 1) % 8, c)
    down = device_at(x, y, (z + 7) % 8, c)
    sib = device_at(x, y, z, 1 - c)

    p_dest = []
    for sq in range(2):
        for hl in range(2):
            xd, yd, cd = 2 * c + hl, 2 * sq + zh, x % 2
            cross = x // 2 != sq
            zd = jnp.where(cross, 7 - z, z)
            same = (xd == x) & (yd == y) & jnp.logical_not(cross) & (cd == c)
            p_dest.append((device_at(xd, yd, zd, cd), same))
    p_src = []
    away = zh != half
    for ys in range(4):
        xs, cs = 2 * jnp.where(away, 1 - seq, seq) + c, x // 2
        zs = jnp.where(away, 7 - z, z)
        same = (xs == x) & (ys == y) & jnp.logical_not(away) & (cs == c)
        p_src.append((device_at(xs, ys, zs, cs), same))
    member = zh == half
    h_dest = []
    for yd in range(2):
        for xd in range(4):
            yy, cd = 2 * yd + c, x // 2
            same = (xd == x) & (yy == y) & (cd == c)
            h_dest.append((device_at(xd, yy, z, cd), same, member & jnp.logical_not(same)))
    h_src = []
    for sq in range(2):
        for hl in range(2):
            xs, ys, cs = 2 * c + hl, 2 * sq + zh, y % 2
            same = (xs == x) & (ys == y) & (cs == c)
            h_src.append((device_at(xs, ys, z, cs), same))

    bar = pltpu.get_barrier_semaphore()

    def greet(where):
        pl.semaphore_signal(bar, inc=1, device_id=where, device_id_type=MESH)

    def greet_column(d, carry):
        greet(column((j + d) % 16))
        return carry

    for where, same in p_src + h_src:

        @pl.when(jnp.logical_not(same))
        def _():
            greet(where)

    lax.fori_loop(1, 16, greet_column, 0)
    for where in (up, down, sib):
        greet(where)
    cps_p = [copy_in(prompt_k, in_pk, sem_in.at[0]), copy_in(prompt_v, in_pv, sem_in.at[1])]
    cps_h = [
        copy_in(a, b, sem_in.at[5 + i])
        for i, (a, b) in enumerate(
            [(owners_h, owners), (hand_q_h, hand_q), (hand_k_h, hand_k), (hand_v_h, hand_v)]
        )
    ]
    cps_s = [
        copy_in(span_k, in_k, sem_in.at[2]),
        copy_in(span_v, in_v, sem_in.at[3]),
        copy_in(span_q, in_q, sem_in.at[4]),
    ]
    cps_d = [
        copy_in(a, b, sem_in.at[9 + i])
        for i, (a, b) in enumerate(
            [(plen_h, plen), (rlen_h, rlen), (dec_q_h, dec_q), (dec_k_h, dec_k), (dec_v_h, dec_v)]
        )
    ]
    cps_k = [copy_in(res_k.at[r], in_rk.at[r], sem_rk.at[r]) for r in range(4)]
    cps_v = [copy_in(res_v.at[r], in_rv.at[r], sem_rv.at[r]) for r in range(4)]

    expect = 18
    for _, same in p_dest:
        expect = expect + jnp.where(same, 0, 1)
    for _, _, go in h_dest:
        expect = expect + jnp.where(go, 1, 0)

    for cp in cps_h:
        cp.wait()
    hq = hand_q[...].astype(F32)
    hkv = jnp.concatenate([hand_k[...].astype(F32), hand_v[...].astype(F32)], axis=0)
    for cp in cps_p:
        cp.wait()
    for sq in range(2):
        wide[2 * sq] = in_pk[sq].astype(F32)
        wide[2 * sq + 1] = in_pv[sq].astype(F32)
    for sq in range(2):
        mine = jnp.where(owners[sq] == s, 1.0, 0.0)
        for hl in range(2):
            k = 2 * sq + hl
            stp[k, 0:64, :] = wide[2 * sq, pl.ds(hl, 64, stride=2), :].astype(BF16)
            stp[k, 64:128, :] = wide[2 * sq + 1, pl.ds(hl, 64, stride=2), :].astype(BF16)
            block = jnp.concatenate([hq[:, 8 * hl : 8 * hl + 8, :].reshape(32, 128), hkv], axis=0)
            stp[k, 128:176, :] = (block * mine).astype(BF16)

    pl.semaphore_wait(bar, expect)

    for k, (where, same) in enumerate(p_dest):

        @pl.when(jnp.logical_not(same))
        def _():
            pltpu.make_async_remote_copy(
                stp.at[k], rcp.at[y], p_send.at[k], p_recv, device_id=where, device_id_type=MESH
            ).start()

        @pl.when(same)
        def _():
            pltpu.make_async_copy(stp.at[k], rcp.at[y], p_recv).start()

    for cp in cps_s:
        cp.wait()
    for sq in range(2):
        wide[sq, 0:64, :] = in_k[sq].astype(F32).reshape(64, 128)
        wide[sq, 64:128, :] = in_v[sq].astype(F32).reshape(64, 128)
    for sq in range(2):
        for h in range(8):
            stn[8 * sq + h] = jnp.concatenate(
                [wide[sq, pl.ds(h, 8, stride=8), :], wide[sq, pl.ds(64 + h, 8, stride=8), :]], axis=0
            ).astype(BF16)

    def send_n(d, carry):
        jj = (j + d) % 16
        pltpu.make_async_remote_copy(
            stn.at[jj], rcn.at[j], n_send, n_recv, device_id=column(jj), device_id_type=MESH
        ).start()
        return carry

    lax.fori_loop(1, 16, send_n, 0)
    pltpu.make_async_copy(stn.at[j], rcn.at[j], n_recv).start()

    for sq in range(2):
        for hh in range(4):
            two = in_q[sq, :, 16 * hh : 16 * hh + 16, :].astype(F32)
            for e in range(2):
                h = 2 * hh + e
                stq[8 * sq + h] = two[:, 8 * e : 8 * e + 8, :].reshape(64, 128).astype(BF16)

    def send_q(d, carry):
        jj = (j + d) % 16
        pltpu.make_async_remote_copy(
            stq.at[jj], rcq.at[j], q_send, q_recv, device_id=column(jj), device_id_type=MESH
        ).start()
        return carry

    lax.fori_loop(1, 16, send_q, 0)
    pltpu.make_async_copy(stq.at[j], rcq.at[j], q_recv).start()

    row = lax.broadcasted_iota(jnp.int32, (1024, 128), 0)
    lane = lax.broadcasted_iota(jnp.int32, (1024, 128), 1)
    dmat[...] = (
        32 * (row // 64) + (row % 64) // 8 - 32 * (lane // 8) - lane % 8
    ).astype(F32)
    top[...] = jnp.full((1024, 128), LOW, F32)
    total[...] = jnp.zeros((1024, 128), F32)
    mixed[...] = jnp.zeros((1024, 128), F32)

    for cp in cps_d:
        cp.wait()
    dkpad[...] = jnp.zeros((128, 128), BF16)
    dvpad[...] = jnp.zeros((128, 128), BF16)
    dkpad[0:32, :] = dec_k[...]
    dvpad[0:32, :] = dec_v[...]
    col = lax.broadcasted_iota(jnp.int32, (8, 2048), 1)
    row64 = lax.broadcasted_iota(jnp.int32, (64, 128), 0)
    lane64 = lax.broadcasted_iota(jnp.int32, (64, 128), 1)
    own_ok = (lane64 % 2 == (row64 // 8) % 2) & ((lane64 % 8) // 2 <= row64 // 16)
    for r in range(4):
        cps_k[r].wait()
        qr = dec_q[r]
        sc = dot_t(qr, in_rk[r])
        inside = col // 2 < rlen[r]
        b0 = jnp.where(inside & (col % 2 == 0), 0.0, LOW)
        b1 = jnp.where(inside & (col % 2 == 1), 0.0, LOW)
        both = jnp.concatenate([b0, b1], axis=0)
        sc = sc + jnp.concatenate([both] * 4, axis=0)
        so = jnp.where(own_ok & (lane64 // 8 == r), dot_t(qr, dkpad[...]), LOW)
        mx = jnp.maximum(jnp.max(sc, axis=1, keepdims=True), jnp.max(so, axis=1, keepdims=True))
        ps = jnp.exp2((sc - mx) * SCALE)
        po = jnp.exp2((so - mx) * SCALE)
        den = jnp.sum(ps, axis=1, keepdims=True) + jnp.sum(po, axis=1, keepdims=True)
        cps_v[r].wait()
        num = dot(ps.astype(BF16), in_rv[r]) + dot(po.astype(BF16), dvpad[...])
        resbuf[r] = (num / den).astype(BF16)
    cp_res = pltpu.make_async_copy(resbuf, out_r, sem_out.at[0])
    cp_res.start()

    def recv(ref, sem):
        pltpu.make_async_remote_copy(ref, ref, h_send.at[0], sem, device_id=sib, device_id_type=MESH).wait_recv()

    parts = (pl.ds(0, 416), pl.ds(416, 400))

    def hop(src, dst, part, where, lane_index):
        pltpu.make_async_remote_copy(
            kv.at[src, c, parts[part]], kv.at[dst, c, parts[part]],
            ring_send.at[lane_index], ring_recv.at[dst, part], device_id=where, device_id_type=MESH,
        ).start()

    def share(slot, part):
        pltpu.make_async_remote_copy(
            kv.at[slot, c, parts[part]], kv.at[slot, c, parts[part]],
            sib_send, sib_recv.at[slot, part], device_id=sib, device_id_type=MESH,
        ).start()

    def arrive(slot, part):
        recv(kv.at[slot, c, parts[part]], ring_recv.at[slot, part])

    def shared(slot):
        for part in (0, 1):
            recv(kv.at[slot, 1 - c, parts[part]], sib_recv.at[slot, part])

    recv(rcp, p_recv)
    handed = rcp[0, 128:176, :].astype(F32)
    for ys in range(4):
        kv[0, c, 64 * ys : 64 * ys + 64, :] = rcp[ys, 0:64, :]
        kv[0, c, 256 + 64 * ys : 320 + 64 * ys, :] = rcp[ys, 64:128, :]
        if ys:
            handed = handed + rcp[ys, 128:176, :].astype(F32)
    kv[0, c, 512:560, :] = handed.astype(BF16)
    hop(0, 1, 0, up, 0)
    hop(0, 2, 0, down, 1)
    share(0, 0)
    recv(rcn, n_recv)
    new = rcn[...].astype(F32)
    kv[0, c, 560:688, :] = new[:, 0:8, :].reshape(128, 128).astype(BF16)
    kv[0, c, 688:816, :] = new[:, 8:16, :].reshape(128, 128).astype(BF16)
    hop(0, 1, 1, up, 0)
    hop(0, 2, 1, down, 1)
    share(0, 1)

    plen_here = plen[seq]
    lane1 = lax.broadcasted_iota(jnp.int32, (1, 128), 1)
    lane_pos = 1024 * (lane1 // 64) + lane1 % 64
    z_of = [z, (z + 7) % 8, (z + 1) % 8, (z + 6) % 8, (z + 2) % 8, (z + 5) % 8, (z + 3) % 8, (z + 4) % 8]

    def prompt_bias(slot, cc):
        zz = z_of[slot]
        near = 256 * (cc + 2 * seq) + 64 * (zz % 4)
        far = 256 * (cc + 2 * (1 - seq)) + 64 * (3 - zz % 4)
        off = jnp.where(zz // 4 == half, near, far)
        return [jnp.where(lane_pos + (off + 2048 * e) < plen_here, 0.0, LOW) for e in range(2)]

    def process(blocks, after=None):
        rows = ROWS if after is not None else 1024
        bias = [prompt_bias(slot, cc) for slot, cc in blocks]
        limit = [
            (512 * (2 * (z_of[slot] // 4) + cc - t) + 8 * (z_of[slot] % 4 - zl)).astype(F32)
            for slot, cc in blocks
        ]

        def tile(n):
            rs = pl.ds(n * rows, rows)
            q = rcq[n * (rows // 64) : (n + 1) * (rows // 64), :, :].reshape(rows, 128)
            keys = jnp.concatenate(
                [kv[slot, cc, part, :] for slot, cc in blocks for part in (slice(0, 256), slice(560, 688))], axis=0
            )
            values = jnp.concatenate(
                [kv[slot, cc, part, :] for slot, cc in blocks for part in (slice(256, 512), slice(688, 816))], axis=0
            )
            sc = dot_t(q, keys)
            ss = []
            for i in range(len(blocks)):
                ss.append(sc[:, 384 * i : 384 * i + 128] + bias[i][0])
                ss.append(sc[:, 384 * i + 128 : 384 * i + 256] + bias[i][1])
                ss.append(jnp.where(dmat[rs, :] >= limit[i], sc[:, 384 * i + 256 : 384 * i + 384], LOW))
            mx = ss[0]
            for v in ss[1:]:
                mx = jnp.maximum(mx, v)
            old = top[rs, :]
            now = jnp.maximum(old, jnp.max(mx, axis=1, keepdims=True))
            shrink = jnp.exp2((old - now) * SCALE)
            top[rs, :] = now
            ps = [jnp.exp2((v - now) * SCALE) for v in ss]
            su = ps[0]
            for v in ps[1:]:
                su = su + v
            p = jnp.concatenate([v.astype(BF16) for v in ps], axis=1)
            mixed[rs, :] = mixed[rs, :] * shrink + dot(p, values)
            total[rs, :] = total[rs, :] * shrink + su

        for n in range(1024 // rows):
            tile(n)
            if after is not None:
                after(n)

    def send_o(n):
        rs = pl.ds(n * ROWS, ROWS)
        count = ROWS // 64
        part = mixed[rs, :] / jnp.sum(total[rs, :], axis=1, keepdims=True)
        sto[n * count : (n + 1) * count] = part.astype(BF16).reshape(count, 64, 128)

        def one(d, carry):
            jj = n * count + (j + d) % count

            @pl.when(jj != j)
            def _():
                pltpu.make_async_remote_copy(
                    sto.at[jj], rco.at[j], o_send, o_recv, device_id=column(jj), device_id_type=MESH
                ).start()

            @pl.when(jj == j)
            def _():
                pltpu.make_async_copy(sto.at[jj], rco.at[j], o_recv).start()

            return carry

        lax.fori_loop(0, count, one, 0)

    def theirs(slots):
        for slot in slots:
            shared(slot)
        process([(slot, 1 - c) for slot in slots])

    recv(rcq, q_recv)
    process([(0, c)])
    for a in (1, 2, 3):
        plus, minus = 2 * a - 1, 2 * a
        for part in (0, 1):
            arrive(plus, part)
            if a < 3:
                hop(plus, plus + 2, part, up, 0)
            elif part == 0:
                hop(plus, 7, part, up, 2)
            arrive(minus, part)
            if a < 3:
                hop(minus, minus + 2, part, down, 1)
            elif part == 1:
                hop(minus, 7, part, down, 3)
            share(plus, part)
            share(minus, part)
            if part == 0:
                theirs([0] if a == 1 else [plus - 2, minus - 2])
        process([(plus, c), (minus, c)])
    arrive(7, 0)
    share(7, 0)
    theirs([5, 6])
    arrive(7, 1)
    share(7, 1)
    process([(7, c)])
    shared(7)
    process([(7, 1 - c)], send_o)

    hsum = jnp.zeros((48, 128), F32)
    for slot in range(8):
        for cc in range(2):
            hsum = hsum + kv[slot, cc, 512:560, :].astype(F32)
    qh = hsum[0:32, :].astype(BF16)
    dkpad[...] = jnp.zeros((128, 128), BF16)
    dvpad[...] = jnp.zeros((128, 128), BF16)
    zero8 = jnp.zeros((8, 128), F32)
    dkpad[0:16, :] = jnp.concatenate([hsum[32:40, :], zero8], axis=0).astype(BF16)
    dvpad[0:16, :] = jnp.concatenate([hsum[40:48, :], zero8], axis=0).astype(BF16)
    row32 = lax.broadcasted_iota(jnp.int32, (32, 128), 0)
    lane32 = lax.broadcasted_iota(jnp.int32, (32, 128), 1)
    ok = (lane32 < 8) & (lane32 % 2 == x % 2) & (lane32 // 2 <= row32 // 8)
    so = jnp.where(ok, dot_t(qh, dkpad[...]), LOW)
    ss = []
    for slot in range(8):
        for cc in range(2):
            sc = dot_t(qh, jnp.concatenate([kv[slot, cc, 0:256, :], kv[slot, cc, 560:688, :]], axis=0))
            bias = prompt_bias(slot, cc)
            ss.append([sc[:, 0:128] + bias[0], sc[:, 128:256] + bias[1], sc[:, 256:384]])
    mx = so
    for three in ss:
        for v in three:
            mx = jnp.maximum(mx, v)
    mx = jnp.max(mx, axis=1, keepdims=True)
    po = jnp.exp2((so - mx) * SCALE)
    su = po
    num = dot(po.astype(BF16), dvpad[...])
    for i, three in enumerate(ss):
        ps = [jnp.exp2((v - mx) * SCALE) for v in three]
        su = su + ps[0] + ps[1] + ps[2]
        p = jnp.concatenate([v.astype(BF16) for v in ps], axis=1)
        num = num + dot(
            p, jnp.concatenate([kv[i // 2, i % 2, 256:512, :], kv[i // 2, i % 2, 688:816, :]], axis=0)
        )
    sth[...] = (num / jnp.sum(su, axis=1, keepdims=True)).astype(BF16)
    slot_h = seq * 2 + x % 2
    for k, (where, same, go) in enumerate(h_dest):

        @pl.when(go)
        def _():
            pltpu.make_async_remote_copy(
                sth, rch.at[slot_h], h_send.at[k], h_recv, device_id=where, device_id_type=MESH
            ).start()

        @pl.when(member & same)
        def _():
            pltpu.make_async_copy(sth, rch.at[slot_h], h_recv).start()

    recv(rch, h_recv)
    heads = []
    for hl in range(2):
        acc = jnp.zeros((32, 128), F32)
        for sq in range(2):
            mine = jnp.where(owners[sq] == s, 1.0, 0.0)
            acc = acc + rch[2 * sq + hl].astype(F32) * mine
        heads.append(acc.reshape(4, 8, 128))
    hbuf[...] = jnp.concatenate(heads, axis=1).astype(BF16)
    cp_hand = pltpu.make_async_copy(hbuf, out_h, sem_out.at[1])
    cp_hand.start()

    recv(rco, o_recv)

    def sent(ref, sem):
        pltpu.make_async_remote_copy(ref, ref, sem, h_recv, device_id=sib, device_id_type=MESH).wait_send()

    for k, (_, same) in enumerate(p_dest):

        @pl.when(jnp.logical_not(same))
        def _():
            sent(stp.at[k], p_send.at[k])

    for k, (_, same, go) in enumerate(h_dest):

        @pl.when(go)
        def _():
            sent(sth, h_send.at[k])

    sent(stn.at[pl.ds(0, 15)], n_send)
    sent(stq.at[pl.ds(0, 15)], q_send)
    sent(sto.at[pl.ds(0, 15)], o_send)
    sent(kv.at[pl.ds(0, 3), 0], ring_send.at[0])
    sent(kv.at[pl.ds(0, 3), 0], ring_send.at[1])
    sent(kv.at[0, 0, parts[0]], ring_send.at[2])
    sent(kv.at[0, 0, parts[1]], ring_send.at[3])
    sent(kv.at[pl.ds(0, 8), 0], sib_send)
    cp_res.wait()
    cp_hand.wait()


def place(got, res, hand, out_p, out_r, out_h, pieces, whole, sem_in, sem_out):
    cp_r = pltpu.make_async_copy(res, out_r, sem_out.at[2])
    cp_h = pltpu.make_async_copy(hand, out_h, sem_out.at[3])
    loads = [
        pltpu.make_async_copy(got.at[pl.ds(8 * sq, 8)], pieces.at[pl.ds(8 * sq, 8)], sem_in.at[sq])
        for sq in range(2)
    ]
    for cp in loads:
        cp.start()
    cp_r.start()
    cp_h.start()
    stores = []
    for sq in range(2):
        loads[sq].wait()
        for hh in range(4):
            a = pieces[8 * sq + 2 * hh].astype(F32).reshape(8, 8, 128)
            b = pieces[8 * sq + 2 * hh + 1].astype(F32).reshape(8, 8, 128)
            whole[sq, :, 16 * hh : 16 * hh + 16, :] = jnp.concatenate([a, b], axis=1).astype(BF16)
        cp = pltpu.make_async_copy(whole.at[sq], out_p.at[sq], sem_out.at[sq])
        cp.start()
        stores.append(cp)
    for cp in stores:
        cp.wait()
    cp_r.wait()
    cp_h.wait()


def on_device(
    prompt_lengths, owners, span_q, span_k, span_v, prompt_keys, prompt_values, res_lengths,
    res_keys, res_values, dec_q, dec_k, dec_v, hand_q, hand_k, hand_v,
):
    hbm = pl.BlockSpec(memory_space=pltpu.HBM)
    dma = pltpu.SemaphoreType.DMA
    out = pl.pallas_call(
        kernel,
        out_shape=(
            jax.ShapeDtypeStruct((16, 64, 128), BF16),
            jax.ShapeDtypeStruct((4, 64, 128), BF16),
            jax.ShapeDtypeStruct((4, 16, 128), BF16),
        ),
        in_specs=[hbm] * 16,
        out_specs=(hbm, hbm, hbm),
        scratch_shapes=[
            pltpu.VMEM((2, 8, 64, 128), BF16),
            pltpu.VMEM((2, 8, 8, 128), BF16),
            pltpu.VMEM((2, 8, 8, 128), BF16),
            pltpu.VMEM((2, 128, 128), BF16),
            pltpu.VMEM((2, 128, 128), BF16),
            pltpu.VMEM((4, 2048, 128), BF16),
            pltpu.VMEM((4, 2048, 128), BF16),
            pltpu.SMEM((2,), jnp.int32),
            pltpu.SMEM((2,), jnp.int32),
            pltpu.SMEM((4,), jnp.int32),
            pltpu.VMEM((4, 64, 128), BF16),
            pltpu.VMEM((32, 128), BF16),
            pltpu.VMEM((32, 128), BF16),
            pltpu.VMEM((4, 16, 128), BF16),
            pltpu.VMEM((8, 128), BF16),
            pltpu.VMEM((8, 128), BF16),
            pltpu.VMEM((4, 16, 128), BF16),
            pltpu.VMEM((4, 128, 128), F32),
            pltpu.VMEM((16, 16, 128), BF16),
            pltpu.VMEM((16, 16, 128), BF16),
            pltpu.VMEM((16, 64, 128), BF16),
            pltpu.VMEM((16, 64, 128), BF16),
            pltpu.VMEM((4, 176, 128), BF16),
            pltpu.VMEM((4, 176, 128), BF16),
            pltpu.VMEM((8, 2, 816, 128), BF16),
            pltpu.VMEM((1024, 128), F32),
            pltpu.VMEM((1024, 128), F32),
            pltpu.VMEM((1024, 128), F32),
            pltpu.VMEM((1024, 128), F32),
            pltpu.VMEM((16, 64, 128), BF16),
            pltpu.VMEM((32, 128), BF16),
            pltpu.VMEM((4, 32, 128), BF16),
            pltpu.VMEM((4, 64, 128), BF16),
            pltpu.VMEM((128, 128), BF16),
            pltpu.VMEM((128, 128), BF16),
            dma((14,)), dma((4,)), dma((4,)), dma((2,)),
            dma, dma, dma, dma, dma((4,)), dma, dma((4,)), dma((8, 2)), dma, dma((8, 2)),
            dma, dma, dma((8,)), dma,
        ],
        compiler_params=pltpu.CompilerParams(
            collective_id=0, has_side_effects=True, vmem_limit_bytes=64 << 20
        ),
        name="spanned",
    )(
        prompt_lengths, owners, res_lengths, span_q, span_k, span_v,
        prompt_keys.reshape(2, 128, 128), prompt_values.reshape(2, 128, 128),
        res_keys.reshape(4, 2048, 128), res_values.reshape(4, 2048, 128),
        dec_q.reshape(4, 64, 128), dec_k.reshape(32, 128), dec_v.reshape(32, 128),
        hand_q.reshape(4, 16, 128), hand_k.reshape(8, 128), hand_v.reshape(8, 128),
    )
    any_space = pl.BlockSpec(memory_space=pl.ANY)
    prefill_out, res_out, hand_out = pl.pallas_call(
        place,
        out_shape=(
            jax.ShapeDtypeStruct((2, 8, 64, 128), BF16),
            jax.ShapeDtypeStruct((4, 64, 128), BF16),
            jax.ShapeDtypeStruct((4, 16, 128), BF16),
        ),
        in_specs=[any_space] * 3,
        out_specs=(any_space,) * 3,
        scratch_shapes=[
            pltpu.VMEM((16, 64, 128), BF16), pltpu.VMEM((2, 8, 64, 128), BF16), dma((2,)), dma((4,)),
        ],
        compiler_params=pltpu.CompilerParams(vmem_limit_bytes=64 << 20),
        name="place",
    )(*out)
    return (prefill_out, res_out.reshape(4, 4, 16, 128), hand_out.reshape(1, 4, 16, 128))


def solution(mesh):
    cache = P("section", None, "tensor", None)
    span = P(None, ("tensor", "section"), None, None)
    prompt = P(None, "section", "tensor", None)
    return jax.shard_map(
        on_device,
        mesh=mesh,
        in_specs=(P(), P(), span, span, span, prompt, prompt, P("section")) + (cache,) * 8,
        out_specs=(span, cache, cache),
        check_vma=False,
    )
```

time: 70.4 us -> 55.4 us (0.79)
  local copies, waits for them, and re-layouts: 12.3 us -> 0 us
  Pallas kernels: 56.8 us -> 54.5 us
    unnamed x31 -> x0, local copies, waits for them, and re-layouts: 12.3 us -> none
    pallas_call x1 -> x2, Pallas kernels: 56.8 us -> 54.5 us  [the longest x1 50.8 us: on_device(): pl.pallas_call(kernel, out_shape=(jax.ShapeDtypeStruct((16, 64, 128), BF1...]
where the time goes in v2:
time: 55.4 us; the launch traced here: 55.3 us
  Pallas kernels  54.5 us (98%)
  between operations  0.81 us (1%)
    pallas_call x1, Pallas kernels, on_device(): pl.pallas_call(kernel, out_shape=(jax.ShapeDtypeStruct((16, 64, 128), BF1...  50.8 us
    pallas_call x1, Pallas kernels, on_device(): pl.pallas_call(place, out_shape=(jax.ShapeDtypeStruct((2, 8, 64, 128), BF...  3.64 us

profile of v2, /device:TPU:1, one launch (start us, length us, event | category | flops | bytes accessed | tf_op | source)
XLA Modules:
  0.0 55.3 jit_solution(3791699466452836586)
XLA Ops:
  0.6 50.8 %spanned.1 = (bf16[16,64,128]{2,1,0:T(8,128)(2,1)}, bf16[4,64,128]{2,1,0:T(8,128)(2,1)}, bf16[4,16,128]{2,1,0:T(8,128)(2,1)}) custom-call(s32[2]{0:T(128)} %plen_h.1, s32[2]{0:T(128)} %owners_h.1, s32[4]{0:T(128)} %rlen_h.1, bf16[2,8,64,128]{3,2,1,0:T(8,128)(2,1)} %span_q.1, bf16[2,8,8,128]{3,2,1,0:T(8,128)(2,1)} %span_k.1, bf16[2,8,8,128]{3,2,1,0:T(8,128)(2,1)} %span_v.1, ...), custom_call_target="tpu_custom_call" | custom-call | tf_op jit(solution)/shard_map/spanned/pallas_call | solution.py:521
  51.5 3.6 %place.1 = (bf16[2,8,64,128]{3,2,1,0:T(8,128)(2,1)}, bf16[4,64,128]{2,1,0:T(8,128)(2,1)}, bf16[4,16,128]{2,1,0:T(8,128)(2,1)}) custom-call(bf16[16,64,128]{2,1,0:T(8,128)(2,1)} %get-tuple-element.9.got, bf16[4,64,128]{2,1,0:T(8,128)(2,1)} %get-tuple-element.10.res, bf16[4,16,128]{2,1,0:T(8,128)(2,1)} %get-tuple-element.11.hand), custom_call_target="tpu_custom_call" | custom-call | tf_op jit(solution)/shard_map/place/pallas_call | solution.py:582

commit v3 on v2

--- a/solution.py
+++ b/solution.py
@@ -86,6 +86,7 @@
             same = (xs == x) & (ys == y) & (cs == c)
             h_src.append((device_at(xs, ys, z, cs), same))
 
+    cps_p = [copy_in(prompt_k, in_pk, sem_in.at[0]), copy_in(prompt_v, in_pv, sem_in.at[1])]
     bar = pltpu.get_barrier_semaphore()
 
     def greet(where):
@@ -104,7 +105,6 @@
     lax.fori_loop(1, 16, greet_column, 0)
     for where in (up, down, sib):
         greet(where)
-    cps_p = [copy_in(prompt_k, in_pk, sem_in.at[0]), copy_in(prompt_v, in_pv, sem_in.at[1])]
     cps_h = [
         copy_in(a, b, sem_in.at[5 + i])
         for i, (a, b) in enumerate(
@@ -243,45 +243,45 @@
     def recv(ref, sem):
         pltpu.make_async_remote_copy(ref, ref, h_send.at[0], sem, device_id=sib, device_id_type=MESH).wait_recv()
 
-    parts = (pl.ds(0, 416), pl.ds(416, 400))
-
-    def hop(src, dst, part, where, lane_index):
+    parts = (pl.ds(0, 256), pl.ds(256, 288), pl.ds(544, 272))
+    last = (pl.ds(0, 256), pl.ds(256, 144), pl.ds(400, 144), pl.ds(544, 272))
+
+    def send_on(src, dst, part, where, lane_index, sem):
         pltpu.make_async_remote_copy(
-            kv.at[src, c, parts[part]], kv.at[dst, c, parts[part]],
-            ring_send.at[lane_index], ring_recv.at[dst, part], device_id=where, device_id_type=MESH,
+            kv.at[src, c, part], kv.at[dst, c, part],
+            ring_send.at[lane_index], ring_recv.at[dst, sem], device_id=where, device_id_type=MESH,
         ).start()
 
     def share(slot, part):
         pltpu.make_async_remote_copy(
-            kv.at[slot, c, parts[part]], kv.at[slot, c, parts[part]],
-            sib_send, sib_recv.at[slot, part], device_id=sib, device_id_type=MESH,
+            kv.at[slot, c, part], kv.at[slot, c, part],
+            sib_send, sib_recv.at[slot], device_id=sib, device_id_type=MESH,
         ).start()
 
-    def arrive(slot, part):
-        recv(kv.at[slot, c, parts[part]], ring_recv.at[slot, part])
+    def arrive(slot, part, sem):
+        recv(kv.at[slot, c, part], ring_recv.at[slot, sem])
 
     def shared(slot):
-        for part in (0, 1):
-            recv(kv.at[slot, 1 - c, parts[part]], sib_recv.at[slot, part])
-
+        recv(kv.at[slot, 1 - c], sib_recv.at[slot])
+
+    recv(rcn, n_recv)
+    new = rcn[...].astype(F32)
+    kv[0, c, 0:128, :] = new[:, 0:8, :].reshape(128, 128).astype(BF16)
+    kv[0, c, 128:256, :] = new[:, 8:16, :].reshape(128, 128).astype(BF16)
+    send_on(0, 1, parts[0], up, 0, 0)
+    send_on(0, 2, parts[0], down, 1, 0)
     recv(rcp, p_recv)
     handed = rcp[0, 128:176, :].astype(F32)
     for ys in range(4):
-        kv[0, c, 64 * ys : 64 * ys + 64, :] = rcp[ys, 0:64, :]
-        kv[0, c, 256 + 64 * ys : 320 + 64 * ys, :] = rcp[ys, 64:128, :]
+        kv[0, c, 256 + 64 * ys : 320 + 64 * ys, :] = rcp[ys, 0:64, :]
+        kv[0, c, 512 + 64 * ys : 576 + 64 * ys, :] = rcp[ys, 64:128, :]
         if ys:
             handed = handed + rcp[ys, 128:176, :].astype(F32)
-    kv[0, c, 512:560, :] = handed.astype(BF16)
-    hop(0, 1, 0, up, 0)
-    hop(0, 2, 0, down, 1)
-    share(0, 0)
-    recv(rcn, n_recv)
-    new = rcn[...].astype(F32)
-    kv[0, c, 560:688, :] = new[:, 0:8, :].reshape(128, 128).astype(BF16)
-    kv[0, c, 688:816, :] = new[:, 8:16, :].reshape(128, 128).astype(BF16)
-    hop(0, 1, 1, up, 0)
-    hop(0, 2, 1, down, 1)
-    share(0, 1)
+    kv[0, c, 768:816, :] = handed.astype(BF16)
+    for part in (1, 2):
+        send_on(0, 1, parts[part], up, 0, part)
+        send_on(0, 2, parts[part], down, 1, part)
+    share(0, pl.ds(0, 816))
 
     plen_here = plen[seq]
     lane1 = lax.broadcasted_iota(jnp.int32, (1, 128), 1)
@@ -307,10 +307,10 @@
             rs = pl.ds(n * rows, rows)
             q = rcq[n * (rows // 64) : (n + 1) * (rows // 64), :, :].reshape(rows, 128)
             keys = jnp.concatenate(
-                [kv[slot, cc, part, :] for slot, cc in blocks for part in (slice(0, 256), slice(560, 688))], axis=0
+                [kv[slot, cc, part, :] for slot, cc in blocks for part in (slice(256, 512), slice(0, 128))], axis=0
             )
             values = jnp.concatenate(
-                [kv[slot, cc, part, :] for slot, cc in blocks for part in (slice(256, 512), slice(688, 816))], axis=0
+                [kv[slot, cc, part, :] for slot, cc in blocks for part in (slice(512, 768), slice(128, 256))], axis=0
             )
             sc = dot_t(q, keys)
             ss = []
@@ -370,27 +370,32 @@
     process([(0, c)])
     for a in (1, 2, 3):
         plus, minus = 2 * a - 1, 2 * a
-        for part in (0, 1):
-            arrive(plus, part)
+        for part in (0, 1, 2):
+            arrive(plus, parts[part], part)
             if a < 3:
-                hop(plus, plus + 2, part, up, 0)
+                send_on(plus, plus + 2, parts[part], up, 0, part)
+            elif part < 2:
+                send_on(plus, 7, last[part], up, 2, part)
+            arrive(minus, parts[part], part)
+            if a < 3:
+                send_on(minus, minus + 2, parts[part], down, 1, part)
+            elif part > 0:
+                send_on(minus, 7, last[part + 1], down, 3, part + 1)
+            if part == 2:
+                share(plus, pl.ds(0, 816))
+                share(minus, pl.ds(0, 816))
+            if part < 2 and a > 1:
+                theirs([2 * a - 3 + part])
             elif part == 0:
-                hop(plus, 7, part, up, 2)
-            arrive(minus, part)
-            if a < 3:
-                hop(minus, minus + 2, part, down, 1)
-            elif part == 1:
-                hop(minus, 7, part, down, 3)
-            share(plus, part)
-            share(minus, part)
-            if part == 0:
-                theirs([0] if a == 1 else [plus - 2, minus - 2])
+                theirs([0])
         process([(plus, c), (minus, c)])
-    arrive(7, 0)
-    share(7, 0)
+    arrive(7, last[0], 0)
+    arrive(7, last[1], 1)
+    share(7, pl.ds(0, 400))
     theirs([5, 6])
-    arrive(7, 1)
-    share(7, 1)
+    arrive(7, last[2], 2)
+    arrive(7, last[3], 3)
+    share(7, pl.ds(400, 416))
     process([(7, c)])
     shared(7)
     process([(7, 1 - c)], send_o)
@@ -398,7 +403,7 @@
     hsum = jnp.zeros((48, 128), F32)
     for slot in range(8):
         for cc in range(2):
-            hsum = hsum + kv[slot, cc, 512:560, :].astype(F32)
+            hsum = hsum + kv[slot, cc, 768:816, :].astype(F32)
     qh = hsum[0:32, :].astype(BF16)
     dkpad[...] = jnp.zeros((128, 128), BF16)
     dvpad[...] = jnp.zeros((128, 128), BF16)
@@ -412,7 +417,7 @@
     ss = []
     for slot in range(8):
         for cc in range(2):
-            sc = dot_t(qh, jnp.concatenate([kv[slot, cc, 0:256, :], kv[slot, cc, 560:688, :]], axis=0))
+            sc = dot_t(qh, jnp.concatenate([kv[slot, cc, 256:512, :], kv[slot, cc, 0:128, :]], axis=0))
             bias = prompt_bias(slot, cc)
             ss.append([sc[:, 0:128] + bias[0], sc[:, 128:256] + bias[1], sc[:, 256:384]])
     mx = so
@@ -428,7 +433,7 @@
         su = su + ps[0] + ps[1] + ps[2]
         p = jnp.concatenate([v.astype(BF16) for v in ps], axis=1)
         num = num + dot(
-            p, jnp.concatenate([kv[i // 2, i % 2, 256:512, :], kv[i // 2, i % 2, 688:816, :]], axis=0)
+            p, jnp.concatenate([kv[i // 2, i % 2, 512:768, :], kv[i // 2, i % 2, 128:256, :]], axis=0)
         )
     sth[...] = (num / jnp.sum(su, axis=1, keepdims=True)).astype(BF16)
     slot_h = seq * 2 + x % 2
@@ -443,6 +448,23 @@
         @pl.when(member & same)
         def _():
             pltpu.make_async_copy(sth, rch.at[slot_h], h_recv).start()
+
+    def sent(ref, sem):
+        pltpu.make_async_remote_copy(ref, ref, sem, h_recv, device_id=sib, device_id_type=MESH).wait_send()
+
+    for k, (_, same) in enumerate(p_dest):
+
+        @pl.when(jnp.logical_not(same))
+        def _():
+            sent(stp.at[k], p_send.at[k])
+
+    sent(stn.at[pl.ds(0, 15)], n_send)
+    sent(stq.at[pl.ds(0, 15)], q_send)
+    sent(kv.at[pl.ds(0, 3), 0], ring_send.at[0])
+    sent(kv.at[pl.ds(0, 3), 0], ring_send.at[1])
+    sent(kv.at[0, 0, pl.ds(0, 400)], ring_send.at[2])
+    sent(kv.at[0, 0, pl.ds(400, 416)], ring_send.at[3])
+    sent(kv.at[pl.ds(0, 8), 0], sib_send)
 
     recv(rch, h_recv)
     heads = []
@@ -458,44 +480,30 @@
 
     recv(rco, o_recv)
 
-    def sent(ref, sem):
-        pltpu.make_async_remote_copy(ref, ref, sem, h_recv, device_id=sib, device_id_type=MESH).wait_send()
-
-    for k, (_, same) in enumerate(p_dest):
-
-        @pl.when(jnp.logical_not(same))
-        def _():
-            sent(stp.at[k], p_send.at[k])
-
     for k, (_, same, go) in enumerate(h_dest):
 
         @pl.when(go)
         def _():
             sent(sth, h_send.at[k])
 
-    sent(stn.at[pl.ds(0, 15)], n_send)
-    sent(stq.at[pl.ds(0, 15)], q_send)
     sent(sto.at[pl.ds(0, 15)], o_send)
-    sent(kv.at[pl.ds(0, 3), 0], ring_send.at[0])
-    sent(kv.at[pl.ds(0, 3), 0], ring_send.at[1])
-    sent(kv.at[0, 0, parts[0]], ring_send.at[2])
-    sent(kv.at[0, 0, parts[1]], ring_send.at[3])
-    sent(kv.at[pl.ds(0, 8), 0], sib_send)
     cp_res.wait()
     cp_hand.wait()
 
 
-def place(got, res, hand, out_p, out_r, out_h, pieces, whole, sem_in, sem_out):
-    cp_r = pltpu.make_async_copy(res, out_r, sem_out.at[2])
-    cp_h = pltpu.make_async_copy(hand, out_h, sem_out.at[3])
+def place(got, res, hand, out_p, out_r, out_h, pieces, whole, vres, vhand, sem_in, sem_out):
+    in_r = pltpu.make_async_copy(res, vres, sem_in.at[2])
+    in_h = pltpu.make_async_copy(hand, vhand, sem_in.at[3])
+    cp_r = pltpu.make_async_copy(vres, out_r, sem_out.at[2])
+    cp_h = pltpu.make_async_copy(vhand, out_h, sem_out.at[3])
     loads = [
         pltpu.make_async_copy(got.at[pl.ds(8 * sq, 8)], pieces.at[pl.ds(8 * sq, 8)], sem_in.at[sq])
         for sq in range(2)
     ]
     for cp in loads:
         cp.start()
-    cp_r.start()
-    cp_h.start()
+    in_r.start()
+    in_h.start()
     stores = []
     for sq in range(2):
         loads[sq].wait()
@@ -506,6 +514,10 @@
         cp = pltpu.make_async_copy(whole.at[sq], out_p.at[sq], sem_out.at[sq])
         cp.start()
         stores.append(cp)
+    in_r.wait()
+    cp_r.start()
+    in_h.wait()
+    cp_h.start()
     for cp in stores:
         cp.wait()
     cp_r.wait()
@@ -564,7 +576,7 @@
             pltpu.VMEM((128, 128), BF16),
             pltpu.VMEM((128, 128), BF16),
             dma((14,)), dma((4,)), dma((4,)), dma((2,)),
-            dma, dma, dma, dma, dma((4,)), dma, dma((4,)), dma((8, 2)), dma, dma((8, 2)),
+            dma, dma, dma, dma, dma((4,)), dma, dma((4,)), dma((8, 4)), dma, dma((8,)),
             dma, dma, dma((8,)), dma,
         ],
         compiler_params=pltpu.CompilerParams(
@@ -589,7 +601,8 @@
         in_specs=[any_space] * 3,
         out_specs=(any_space,) * 3,
         scratch_shapes=[
-            pltpu.VMEM((16, 64, 128), BF16), pltpu.VMEM((2, 8, 64, 128), BF16), dma((2,)), dma((4,)),
+            pltpu.VMEM((16, 64, 128), BF16), pltpu.VMEM((2, 8, 64, 128), BF16), pltpu.VMEM((4, 64, 128), BF16),
+            pltpu.VMEM((4, 16, 128), BF16), dma((4,)), dma((4,)),
         ],
         compiler_params=pltpu.CompilerParams(vmem_limit_bytes=64 << 20),
         name="place",

time: 55.4 us -> 52 us (0.939)
  Pallas kernels: 54.5 us -> 51.1 us
    pallas_call x1, Pallas kernels: 3.64 us -> 1.74 us  [on_device(): pl.pallas_call(place, out_shape=(jax.ShapeDtypeStruct((2, 8, 64, 128), BF...]
    pallas_call x1, Pallas kernels: 50.8 us -> 49.3 us  [on_device(): pl.pallas_call(kernel, out_shape=(jax.ShapeDtypeStruct((16, 64, 128), BF1...]
where the time goes in v3:
time: 52 us; the launch traced here: 51.9 us
  Pallas kernels  51.1 us (98%)
  between operations  0.81 us (2%)
    pallas_call x1, Pallas kernels, on_device(): pl.pallas_call(kernel, out_shape=(jax.ShapeDtypeStruct((16, 64, 128), BF1...  49.3 us
    pallas_call x1, Pallas kernels, on_device(): pl.pallas_call(place, out_shape=(jax.ShapeDtypeStruct((2, 8, 64, 128), BF...  1.74 us

profile of v3, /device:TPU:1, one launch (start us, length us, event | category | flops | bytes accessed | tf_op | source)
XLA Modules:
  0.0 51.9 jit_solution(2455045593729824225)
XLA Ops:
  0.6 49.3 %spanned.1 = (bf16[16,64,128]{2,1,0:T(8,128)(2,1)}, bf16[4,64,128]{2,1,0:T(8,128)(2,1)}, bf16[4,16,128]{2,1,0:T(8,128)(2,1)}) custom-call(s32[2]{0:T(128)} %plen_h.1, s32[2]{0:T(128)} %owners_h.1, s32[4]{0:T(128)} %rlen_h.1, bf16[2,8,64,128]{3,2,1,0:T(8,128)(2,1)} %span_q.1, bf16[2,8,8,128]{3,2,1,0:T(8,128)(2,1)} %span_k.1, bf16[2,8,8,128]{3,2,1,0:T(8,128)(2,1)} %span_v.1, ...), custom_call_target="tpu_custom_call" | custom-call | tf_op jit(solution)/shard_map/spanned/pallas_call | solution.py:533
  50.0 1.7 %place.1 = (bf16[2,8,64,128]{3,2,1,0:T(8,128)(2,1)}, bf16[4,64,128]{2,1,0:T(8,128)(2,1)}, bf16[4,16,128]{2,1,0:T(8,128)(2,1)}) custom-call(bf16[16,64,128]{2,1,0:T(8,128)(2,1)} %get-tuple-element.9.got, bf16[4,64,128]{2,1,0:T(8,128)(2,1)} %get-tuple-element.10.res, bf16[4,16,128]{2,1,0:T(8,128)(2,1)} %get-tuple-element.11.hand), custom_call_target="tpu_custom_call" | custom-call | tf_op jit(solution)/shard_map/place/pallas_call | solution.py:594

commit v4 on v3

--- a/solution.py
+++ b/solution.py
@@ -87,30 +87,30 @@
             h_src.append((device_at(xs, ys, z, cs), same))
 
     cps_p = [copy_in(prompt_k, in_pk, sem_in.at[0]), copy_in(prompt_v, in_pv, sem_in.at[1])]
-    bar = pltpu.get_barrier_semaphore()
-
-    def greet(where):
-        pl.semaphore_signal(bar, inc=1, device_id=where, device_id_type=MESH)
-
-    def greet_column(d, carry):
-        greet(column((j + d) % 16))
-        return carry
-
-    for where, same in p_src + h_src:
-
-        @pl.when(jnp.logical_not(same))
-        def _():
-            greet(where)
-
-    lax.fori_loop(1, 16, greet_column, 0)
-    for where in (up, down, sib):
-        greet(where)
     cps_h = [
         copy_in(a, b, sem_in.at[5 + i])
         for i, (a, b) in enumerate(
             [(owners_h, owners), (hand_q_h, hand_q), (hand_k_h, hand_k), (hand_v_h, hand_v)]
         )
     ]
+    bar = pltpu.get_barrier_semaphore()
+
+    def greet(where):
+        pl.semaphore_signal(bar, inc=1, device_id=where, device_id_type=MESH)
+
+    def greet_column(d, carry):
+        greet(column((j + d) % 16))
+        return carry
+
+    for where, same in p_src + h_src:
+
+        @pl.when(jnp.logical_not(same))
+        def _():
+            greet(where)
+
+    lax.fori_loop(1, 16, greet_column, 0)
+    for where in (up, down, sib):
+        greet(where)
     cps_s = [
         copy_in(span_k, in_k, sem_in.at[2]),
         copy_in(span_v, in_v, sem_in.at[3]),
@@ -296,23 +296,25 @@
         return [jnp.where(lane_pos + (off + 2048 * e) < plen_here, 0.0, LOW) for e in range(2)]
 
     def process(blocks, after=None):
-        rows = ROWS if after is not None else 1024
+        rows = 1024 if after is None and len(blocks) == 1 else ROWS
         bias = [prompt_bias(slot, cc) for slot, cc in blocks]
         limit = [
             (512 * (2 * (z_of[slot] // 4) + cc - t) + 8 * (z_of[slot] % 4 - zl)).astype(F32)
             for slot, cc in blocks
         ]
 
-        def tile(n):
+        keys = jnp.concatenate(
+            [kv[slot, cc, part, :] for slot, cc in blocks for part in (slice(256, 512), slice(0, 128))], axis=0
+        )
+        values = jnp.concatenate(
+            [kv[slot, cc, part, :] for slot, cc in blocks for part in (slice(512, 768), slice(128, 256))], axis=0
+        )
+
+        def scores(n):
+            return dot_t(rcq[n * (rows // 64) : (n + 1) * (rows // 64), :, :].reshape(rows, 128), keys)
+
+        def weigh(n, sc):
             rs = pl.ds(n * rows, rows)
-            q = rcq[n * (rows // 64) : (n + 1) * (rows // 64), :, :].reshape(rows, 128)
-            keys = jnp.concatenate(
-                [kv[slot, cc, part, :] for slot, cc in blocks for part in (slice(256, 512), slice(0, 128))], axis=0
-            )
-            values = jnp.concatenate(
-                [kv[slot, cc, part, :] for slot, cc in blocks for part in (slice(512, 768), slice(128, 256))], axis=0
-            )
-            sc = dot_t(q, keys)
             ss = []
             for i in range(len(blocks)):
                 ss.append(sc[:, 384 * i : 384 * i + 128] + bias[i][0])
@@ -329,14 +331,18 @@
             su = ps[0]
             for v in ps[1:]:
                 su = su + v
-            p = jnp.concatenate([v.astype(BF16) for v in ps], axis=1)
+            total[rs, :] = total[rs, :] * shrink + su
+            return shrink, jnp.concatenate([v.astype(BF16) for v in ps], axis=1)
+
+        sc = scores(0)
+        for n in range(1024 // rows):
+            nxt = scores(n + 1) if n + 1 < 1024 // rows else None
+            shrink, p = weigh(n, sc)
+            rs = pl.ds(n * rows, rows)
             mixed[rs, :] = mixed[rs, :] * shrink + dot(p, values)
-            total[rs, :] = total[rs, :] * shrink + su
-
-        for n in range(1024 // rows):
-            tile(n)
             if after is not None:
                 after(n)
+            sc = nxt
 
     def send_o(n):
         rs = pl.ds(n * ROWS, ROWS)

time: 52 us -> 51.3 us (0.987)
  Pallas kernels: 51.1 us -> 50.5 us
    pallas_call x1, Pallas kernels: 49.3 us -> 48.8 us  [on_device(): pl.pallas_call(kernel, out_shape=(jax.ShapeDtypeStruct((16, 64, 128), BF1...]
where the time goes in v4:
time: 51.3 us; the launch traced here: 51.2 us
  Pallas kernels  50.5 us (98%)
  between operations  0.65 us (1%)
    pallas_call x1, Pallas kernels, on_device(): pl.pallas_call(kernel, out_shape=(jax.ShapeDtypeStruct((16, 64, 128), BF1...  48.8 us
    pallas_call x1, Pallas kernels, on_device(): pl.pallas_call(place, out_shape=(jax.ShapeDtypeStruct((2, 8, 64, 128), BF...  1.74 us

profile of v4, /device:TPU:1, one launch (start us, length us, event | category | flops | bytes accessed | tf_op | source)
XLA Modules:
  0.0 51.2 jit_solution(14627174623713492425)
XLA Ops:
  0.6 48.8 %spanned.1 = (bf16[16,64,128]{2,1,0:T(8,128)(2,1)}, bf16[4,64,128]{2,1,0:T(8,128)(2,1)}, bf16[4,16,128]{2,1,0:T(8,128)(2,1)}) custom-call(s32[2]{0:T(128)} %plen_h.1, s32[2]{0:T(128)} %owners_h.1, s32[4]{0:T(128)} %rlen_h.1, bf16[2,8,64,128]{3,2,1,0:T(8,128)(2,1)} %span_q.1, bf16[2,8,8,128]{3,2,1,0:T(8,128)(2,1)} %span_k.1, bf16[2,8,8,128]{3,2,1,0:T(8,128)(2,1)} %span_v.1, ...), custom_call_target="tpu_custom_call" | custom-call | tf_op jit(solution)/shard_map/spanned/pallas_call | solution.py:539
  49.4 1.7 %place.1 = (bf16[2,8,64,128]{3,2,1,0:T(8,128)(2,1)}, bf16[4,64,128]{2,1,0:T(8,128)(2,1)}, bf16[4,16,128]{2,1,0:T(8,128)(2,1)}) custom-call(bf16[16,64,128]{2,1,0:T(8,128)(2,1)} %get-tuple-element.9.got, bf16[4,64,128]{2,1,0:T(8,128)(2,1)} %get-tuple-element.10.res, bf16[4,16,128]{2,1,0:T(8,128)(2,1)} %get-tuple-element.11.hand), custom_call_target="tpu_custom_call" | custom-call | tf_op jit(solution)/shard_map/place/pallas_call | solution.py:600
